TPU v7x, 256 devices: a whole 4x4x8 slice. The times are simulated.
256 devices in a mesh: px: 16 (over y, x), py: 16 (over z, core).
Axes of the slice: x: 4, y: 4, z: 8, core: 2. Of those that a mesh axis runs over, the one named last changes fastest.
Arguments:
- field: bfloat16 [2, 16, 256, 256, 256], P(None, None, 'px', 'py'), may hold values from -6 to 6
- spectral_weight: float32 [16, 16, 2, 16, 16, 16], P('px', 'py'), may hold values from -1 to 1
- skip_weight: bfloat16 [16, 16], replicated, may hold values from -1.5 to 1.5
- bias: float32 [16], replicated, may hold values from -3 to 3
Outputs:
- output: bfloat16 [2, 16, 256, 256, 256], P(None, None, 'px', 'py')
All inputs are finite; a program needn't handle non-finite values.
Results may differ from a plain program's by a relative error of at most 0.014.
Values may be sent and summed in bfloat16 or wider, within the bound.
No kernel may reach another device: no remote copies, remote signals or barrier semaphores. Data moves between devices by JAX's collectives and lax.ppermute only.
A program may use at most 128 MiB of HBM per device.

v0:
```python
import math

import jax
import jax.numpy as jnp
import numpy as np
from jax import lax
from jax.experimental import pallas as pl
from jax.experimental.pallas import tpu as pltpu
from jax.sharding import PartitionSpec as P

GRID = 256
CHANNELS = 16
MODES = 16
SLICES = 2
BLOCK = 16
RANK = 8
HALF = RANK * MODES
LANES = 2 * HALF
Z_CHIPS = 8
VMEM = 48 * 1024 * 1024
CENTRE = (BLOCK - 1) / 2


def make_tables():
    freq = np.concatenate([np.arange(8), np.arange(-8, 0)]).astype(np.float64)
    turn = 2.0 * np.pi / GRID
    u = np.arange(BLOCK) - CENTRE
    basis, weight = [], []
    for part in (np.cos(np.outer(u, turn * freq)), np.sin(np.outer(u, turn * freq))):
        left, scale, right = np.linalg.svd(part)
        basis.append(left[:, :4])
        weight.append(scale[:4, None] * right[:4])
    basis = np.concatenate(basis, axis=1)
    weight = np.concatenate(weight, axis=0)
    odd = np.arange(RANK) >= 4

    kz, z = np.arange(MODES), np.arange(GRID)
    angle = turn * np.outer(z, kz)
    depth = np.stack([np.cos(angle), -np.sin(angle)], axis=1)
    forward_z = np.repeat(depth[:, :, None, :], RANK, axis=2).reshape(GRID, LANES)
    w = np.where(kz == 0, 1.0, 2.0) * (0.5 / math.sqrt(MODES**3))
    inverse_z = np.repeat((depth * w)[:, :, None, :], RANK, axis=2).reshape(GRID, LANES).T
    lanes_x = np.tile(np.repeat(basis, MODES, axis=1), (1, 2))

    forward_y = np.zeros((16, 16, 2, 16, 16))
    inverse_y = np.zeros((16, 16, 2, 16, 16))
    scale = float(GRID) ** -1.5
    for q in range(16):
        for s in range(2):
            for chip in range(Z_CHIPS):
                theta = turn * freq[2 * chip + ((q % 2) ^ s)] * (16 * q + np.arange(16))
                row = s * Z_CHIPS + chip
                forward_y[q, row, 0] = (np.cos(theta) * scale)[None, :]
                forward_y[q, row, 1] = (np.sin(theta) * scale)[None, :]
                inverse_y[q, :, 0, row] = np.cos(theta)[:, None]
                inverse_y[q, :, 1, row] = -np.sin(theta)[:, None]

    phase = turn * np.outer(freq, 16 * np.arange(16) + CENTRE)
    forward_x = np.stack([np.cos(phase), np.sin(phase)], axis=1)
    forward_x = np.repeat(forward_x[..., None], CHANNELS, axis=3).reshape(16, 512)
    lanes_v = np.tile(np.repeat(weight.T, MODES, axis=1), (1, 2))
    inverse_x = np.zeros((16, 2, RANK, 2, MODES))
    for p in range(16):
        cos, sin = np.cos(phase[:, p]) * weight, np.sin(phase[:, p]) * weight
        real, imag = np.stack([cos, -sin], axis=1), np.stack([sin, cos], axis=1)
        turned = odd[:, None, None]
        inverse_x[p, 0] = np.where(turned, -imag, real)
        inverse_x[p, 1] = np.where(turned, real, imag)
    inverse_x = inverse_x.reshape(16, 16, 32)

    eye = np.eye(MODES)
    fold = np.zeros((2, RANK, MODES, 2, 8, MODES))
    for r in range(RANK):
        for a in range(2):
            if odd[r]:
                fold[a, r, :, 1 - a] = (1.0 if a else -1.0) * eye[:, None, :]
            else:
                fold[a, r, :, a] = eye[:, None, :]
    fold = fold.reshape(LANES, LANES)
    spread = np.zeros((RANK, 8, MODES, RANK, MODES))
    for r in range(RANK):
        spread[r, :, :, r, :] = eye[None]
    spread = spread.reshape(RANK * 128, 128)

    f32, bf16 = np.float32, jnp.bfloat16
    return dict(
        forward_z=forward_z.astype(f32),
        inverse_z=inverse_z.astype(f32).astype(bf16),
        lanes_x=lanes_x.astype(f32),
        forward_y=forward_y.reshape(16, 16, 512).astype(f32),
        inverse_y=inverse_y.reshape(16, 16, 512).astype(f32),
        forward_x=forward_x.astype(f32),
        lanes_v=lanes_v.astype(f32),
        inverse_x=inverse_x.astype(f32),
        fold=fold.astype(f32).astype(bf16),
        spread=spread.astype(f32).astype(bf16),
    )


def iota(shape, dim):
    return lax.broadcasted_iota(jnp.int32, shape, dim)


def dot(a, b):
    return jnp.dot(a, b, preferred_element_type=jnp.float32)


def repeat_rows(table):
    rows, lanes = table.shape
    return jnp.broadcast_to(table[:, None, :], (rows, 16, lanes)).reshape(rows * 16, lanes)


def tile_rows(table):
    rows, lanes = table.shape
    return jnp.broadcast_to(table[None], (16, rows, lanes)).reshape(rows * 16, lanes)


def masked(table, keep):
    return jnp.where(keep, table, 0.0).astype(jnp.bfloat16)


def turned(data):
    return jnp.concatenate([data[:, HALF:], -data[:, :HALF]], axis=1)


def with_turned(data):
    return jnp.concatenate([data, turned(data)], axis=0).astype(jnp.bfloat16)


def forward_kernel(
    index_ref, field_ref, weight_ref, table_z_ref, lanes_x_ref, table_y_ref,
    keep_ref, send_ref, packed_ref, held, total, arrived,
):
    def fetch(x):
        return pltpu.make_async_copy(field_ref.at[:, :, x], held.at[x], arrived.at[x])

    for x in range(BLOCK):
        fetch(x).start()

    place = (iota((MODES, LANES), 0) == iota((MODES, LANES), 1) % MODES).astype(jnp.bfloat16)
    wide = dot(weight_ref[...].astype(jnp.bfloat16), place)
    rows = iota((512, LANES), 0) % 16
    wide = masked(wide, rows == iota((512, LANES), 1) // MODES)
    gather = (iota((32, 512), 0) == iota((32, 512), 1) // 16).astype(jnp.bfloat16)
    packed_ref[...] = dot(gather, wide).astype(jnp.bfloat16)

    shape = (256, 512)
    table_y = masked(
        repeat_rows(table_y_ref[index_ref[0]]), iota(shape, 0) % 16 == iota(shape, 1) % 256 // 16
    )

    group = 4
    for start in range(0, BLOCK, group):
        for x in range(start, start + group):
            fetch(x).wait()
        data = jnp.concatenate(
            [held[x].reshape(SLICES * 256, GRID) for x in range(start, start + group)], axis=1
        )
        table = jnp.concatenate(
            [
                (table_z_ref[...] * lanes_x_ref[x : x + 1, :]).astype(jnp.bfloat16)
                for x in range(start, start + group)
            ],
            axis=0,
        )
        part = dot(data, table)
        total[...] = part if start == 0 else total[...] + part

    for b in range(SLICES):
        sums = dot(table_y, with_turned(total[b * 256 : (b + 1) * 256, :]))
        sums = sums.reshape(2, Z_CHIPS, CHANNELS, LANES)
        keep_ref[:, b] = sums[0]
        send_ref[:, b] = sums[1].astype(jnp.bfloat16)


def sum_kernel(parts_ref, packed_ref, out_ref):
    parts = parts_ref[...].astype(jnp.float32)
    sums = jnp.sum(parts, axis=0).reshape(32, LANES).astype(jnp.bfloat16)
    message = jnp.concatenate([sums, packed_ref[...]], axis=0)
    out_ref[...] = jnp.broadcast_to(message[None], out_ref.shape)


def mix_kernel(
    index_ref, got_ref, table_x_ref, lanes_v_ref, fold_ref, back_x_ref, spread_ref, out_ref,
):
    shape = (256, 512)
    table_x = masked(repeat_rows(table_x_ref[...]), iota(shape, 0) % 16 == iota(shape, 1) % 16)
    scale = repeat_rows(lanes_v_ref[...])
    mixed = []
    for b in range(SLICES):
        data = got_ref[:, b * 16 : (b + 1) * 16, :].reshape(256, LANES).astype(jnp.float32)
        modes = dot(table_x, with_turned(data)) * scale
        modes = dot(modes.astype(jnp.bfloat16), fold_ref[...]).reshape(MODES, CHANNELS, LANES)
        real, imag = modes[..., :HALF], modes[..., HALF:]
        for h in range(2):
            lanes = slice(h * HALF, (h + 1) * HALF)
            w_real = got_ref[:, 32:48, lanes].astype(jnp.float32)
            w_imag = got_ref[:, 48:64, lanes].astype(jnp.float32)
            out_real = jnp.sum(real * w_real - imag * w_imag, axis=1)
            out_imag = jnp.sum(real * w_imag + imag * w_real, axis=1)
            mixed.append(jnp.concatenate([out_real, out_imag], axis=0))
    mixed = jnp.concatenate(mixed, axis=1)
    mixed = mixed.astype(jnp.bfloat16).astype(jnp.float32)
    back = jnp.dot(
        back_x_ref[index_ref[0]], mixed, precision=lax.Precision.HIGHEST, preferred_element_type=jnp.float32
    )
    own = iota((8, 128), 0) == iota((8, 128), 1) // MODES
    rows = []
    for b in range(SLICES):
        for h in range(2):
            at = (2 * b + h) * 128
            for a in range(2):
                pieces = [
                    jnp.where(own, back[a * RANK + r : a * RANK + r + 1, at : at + 128], 0.0)
                    for r in range(RANK)
                ]
                rows.append(jnp.concatenate(pieces, axis=1))
    rows = jnp.concatenate(rows, axis=0).astype(jnp.bfloat16)
    rows = dot(rows, spread_ref[...]).reshape(SLICES, 2, 2, 8, HALF)
    for b in range(SLICES):
        half = [jnp.concatenate([rows[b, 0, a], rows[b, 1, a]], axis=0) for a in range(2)]
        message = jnp.concatenate(half, axis=1).astype(jnp.bfloat16)
        out_ref[:, b] = jnp.broadcast_to(message[None], (Z_CHIPS, CHANNELS, LANES))


def inverse_kernel(
    index_ref, field_ref, skip_ref, bias_ref, own_ref, other_ref, table_y_ref, table_z_ref, lanes_x_ref,
    out_ref, held, ready, left, bias, modes, arrived, sent,
):
    def fetch(x):
        return pltpu.make_async_copy(field_ref.at[:, :, x], held.at[x], arrived.at[x])

    def store(x):
        return pltpu.make_async_copy(ready.at[x], out_ref.at[:, :, x], sent.at[x])

    for x in range(BLOCK):
        fetch(x).start()

    shape = (256, 512)
    table_y = masked(
        tile_rows(table_y_ref[index_ref[0]]), iota(shape, 0) // 16 == iota(shape, 1) % 16
    )
    for b in range(SLICES):
        data = [ref[:, b].reshape(128, LANES) for ref in (own_ref, other_ref)]
        data = jnp.concatenate(data, axis=0).astype(jnp.float32)
        modes[b] = dot(table_y, with_turned(data))

    shape = (256, 256)
    place = (iota((16, 256), 0) == iota((16, 256), 1) // 16).astype(jnp.bfloat16)
    skip = repeat_rows(dot(skip_ref[...], place))
    left[...] = masked(skip, iota(shape, 0) % 16 == iota(shape, 1) % 16)
    one = iota((256, 16), 0) // 16 == iota((256, 16), 1)
    column = jnp.sum(jnp.where(one, bias_ref[...], 0.0), axis=1, keepdims=True)
    bias[...] = jnp.broadcast_to(column, bias.shape)

    def step(x, carry):
        fetch(x).wait()
        lanes = lanes_x_ref[pl.ds(x, 1), :]
        for b in range(SLICES):
            a = jnp.concatenate([left[...], (modes[b] * lanes).astype(jnp.bfloat16)], axis=1)
            c = jnp.concatenate([held[x, b].reshape(256, GRID), table_z_ref[...]], axis=0)
            value = dot(a, c) + bias[...]
            value = 0.5 * value * (1.0 + lax.erf(value * math.sqrt(0.5)))
            ready[x, b] = value.astype(jnp.bfloat16).reshape(CHANNELS, BLOCK, GRID)
        store(x).start()
        return carry

    lax.fori_loop(0, BLOCK, step, 0)
    for x in range(BLOCK):
        store(x).wait()


VM = pl.BlockSpec(memory_space=pltpu.VMEM)
SM = pl.BlockSpec(memory_space=pltpu.SMEM)
ANY = pl.BlockSpec(memory_space=pl.ANY)
PARAMS = pltpu.CompilerParams(vmem_limit_bytes=VMEM)
PAIR = [(i, i ^ 1) for i in range(16)]
CHIPS = [list(range(0, 16, 2)), list(range(1, 16, 2))]


def shape_of(shape, dtype):
    return jax.ShapeDtypeStruct(shape, dtype)


def on_device(field, spectral_weight, skip_weight, bias):
    t = make_tables()
    f32, bf16 = jnp.float32, jnp.bfloat16
    p = lax.axis_index("px").astype(jnp.int32).reshape(1)
    q = lax.axis_index("py").astype(jnp.int32).reshape(1)
    block = (SLICES, CHANNELS, BLOCK, GRID)
    part = (Z_CHIPS, SLICES, CHANNELS, LANES)

    keep, send, packed = pl.pallas_call(
        forward_kernel,
        name="forward",
        in_specs=[SM, ANY, VM, VM, VM, VM],
        out_specs=[VM, VM, VM],
        out_shape=[shape_of(part, f32), shape_of(part, bf16), shape_of((32, LANES), bf16)],
        scratch_shapes=[
            pltpu.VMEM((BLOCK, *block), bf16),
            pltpu.VMEM((512, LANES), f32),
            pltpu.SemaphoreType.DMA((BLOCK,)),
        ],
        compiler_params=PARAMS,
    )(q, field, spectral_weight.reshape(512, MODES), t["forward_z"], t["lanes_x"], t["forward_y"])
    got = lax.ppermute(send, "py", PAIR)
    sums = (keep + got.astype(f32)).astype(bf16)
    sums = lax.all_to_all(sums, "py", 0, 0, axis_index_groups=CHIPS, tiled=True)
    message = pl.pallas_call(
        sum_kernel,
        name="sum",
        in_specs=[VM, VM],
        out_specs=VM,
        out_shape=shape_of((16, 64, LANES), bf16),
        compiler_params=PARAMS,
    )(sums, packed)
    message = lax.all_to_all(message, "px", 0, 0, tiled=True)
    message = pl.pallas_call(
        mix_kernel,
        name="mix",
        in_specs=[SM, VM, VM, VM, VM, VM, VM],
        out_specs=VM,
        out_shape=shape_of(part, bf16),
        compiler_params=PARAMS,
    )(p, message, t["forward_x"], t["lanes_v"], t["fold"], t["inverse_x"], t["spread"])
    own = lax.all_to_all(message, "py", 0, 0, axis_index_groups=CHIPS, tiled=True)
    other = lax.ppermute(own, "py", PAIR)
    return pl.pallas_call(
        inverse_kernel,
        name="inverse",
        in_specs=[SM, ANY, VM, VM, VM, VM, VM, VM, VM],
        out_specs=ANY,
        out_shape=shape_of(field.shape, bf16),
        scratch_shapes=[
            pltpu.VMEM((BLOCK, *block), bf16),
            pltpu.VMEM((BLOCK, *block), bf16),
            pltpu.VMEM((256, 256), bf16),
            pltpu.VMEM((256, GRID), f32),
            pltpu.VMEM((SLICES, 256, LANES), f32),
            pltpu.SemaphoreType.DMA((BLOCK,)),
            pltpu.SemaphoreType.DMA((BLOCK,)),
        ],
        compiler_params=PARAMS,
    )(q, field, skip_weight, bias.reshape(1, 16), own, other, t["inverse_y"], t["inverse_z"], t["lanes_x"])


def solution(mesh):
    return jax.shard_map(
        on_device,
        mesh=mesh,
        in_specs=(P(None, None, "px", "py", None), P("px", "py", None, None, None, None), P(), P()),
        out_specs=P(None, None, "px", "py", None),
        check_vma=False,
    )
```

profile of v0, /device:TPU:1, one launch (start us, length us, event | category | flops | bytes accessed | tf_op | source)
XLA Modules:
  0.0 71.2 jit_solution(4429964593427181536)
XLA Ops:
  0.0 2.2 %copy-done = bf16[2,16,16,16,256]{4,3,2,1,0:T(8,128)(2,1)S(1)} copy-done((bf16[2,16,16,16,256]{4,3,2,1,0:T(8,128)(2,1)S(1)}, bf16[2,16,16,16,256]{4,3,2,1,0:T(8,128)(2,1)}, u32[]{:S(2)}) %copy-start) | copy-done | bytes 4194328
  2.2 1.0 %copy-done.3 = f32[16,16,512]{2,1,0:T(8,128)S(1)} copy-done((f32[16,16,512]{2,1,0:T(8,128)S(1)}, f32[16,16,512]{2,1,0:T(8,128)}, u32[]{:S(2)}) %copy-start.3) | copy-done | bytes 524312
  3.2 0.9 %copy-done.5 = f32[1,1,2,16,16,16]{5,4,3,2,1,0:T(8,128)S(1)} copy-done((f32[1,1,2,16,16,16]{5,4,3,2,1,0:T(8,128)S(1)}, f32[1,1,2,16,16,16]{5,4,3,2,1,0:T(8,128)}, u32[]{:S(2)}) %copy-start.5) | copy-done | bytes 32792
  4.2 0.9 %copy-done.6 = f32[256,256]{1,0:T(8,128)S(1)} copy-done((f32[256,256]{1,0:T(8,128)S(1)}, f32[256,256]{1,0:T(8,128)}, u32[]{:S(2)}) %copy-start.6) | copy-done | bytes 262168
  5.1 0.7 %copy-done.10 = f32[16,256]{1,0:T(8,128)S(1)} copy-done((f32[16,256]{1,0:T(8,128)S(1)}, f32[16,256]{1,0:T(8,128)}, u32[]{:S(2)}) %copy-start.10) | copy-done | bytes 16408
  5.9 0.0 copy-start.13
  5.9 0.0 copy-start.2
  5.9 0.0 copy-start.7
  5.9 0.0 copy-start.11
  5.9 0.0 copy-start.14
  5.9 0.0 copy-start.15
  5.9 3.3 %forward.1 = (f32[8,2,16,256]{3,2,1,0:T(8,128)S(1)}, bf16[8,2,16,256]{3,2,1,0:T(8,128)(2,1)S(1)}, bf16[32,256]{1,0:T(8,128)(2,1)S(1)}) custom-call(s32[1]{0:T(128)} %bitcast.index_ref, bf16[2,16,16,16,256]{4,3,2,1,0:T(8,128)(2,1)S(1)} %copy-done, f32[512,16]{1,0:T(8,128)S(1)} %bitcast.4, f32[256,256]{1,0:T(8,128)S(1)} %copy-done.6, ...), custom_call_target="tpu_custom_call" | custom-call | tf_op jit(solution)/shard_map/forward/pallas_call | solution.py:293
  9.3 3.3 %collective-permute-start = (bf16[8,2,16,256]{3,2,1,0:T(8,128)(2,1)S(1)}, bf16[8,2,16,256]{3,2,1,0:T(8,128)(2,1)S(1)}, u32[]{:S(2)}, u32[]{:S(2)}) collective-permute-start(bf16[8,2,16,256]{3,2,1,0:T(8,128)(2,1)S(1)} %get-tuple-element.9), channel_id=1, source_target_pairs={{0,1},{1,0},{2,3},{3,2},{4,5},{5,4},{6,7},{7,6},{8,9},{9,8},{10,11... | collective-permute-start | bytes 393224 | tf_op jit(solution)/shard_map/ppermute | solution.py:306
  12.6 1.0 %collective-permute-done = bf16[8,2,16,256]{3,2,1,0:T(8,128)(2,1)S(1)} collective-permute-done((bf16[8,2,16,256]{3,2,1,0:T(8,128)(2,1)S(1)}, bf16[8,2,16,256]{3,2,1,0:T(8,128)(2,1)S(1)}, u32[]{:S(2)}, u32[]{:S(2)}) %collective-permute-start) | collective-permute-done | bytes 131104 | tf_op jit(solution)/shard_map/ppermute | solution.py:306
  13.6 14.1 %all_to_all.15.parts_ref = bf16[8,2,16,256]{3,2,1,0:T(8,128)(2,1)S(1)} all-to-all(bf16[8,2,16,256]{3,2,1,0:T(8,128)(2,1)S(1)} %add_convert_fusion), channel_id=1, replica_groups={{0,2,4,6,8,10,12,14},{1,3,5,7,9,11,13,15},{16,18,20,22,24,26,28,30},{17..., dimensions={0} | all-to-all | bytes 262144 | tf_op jit(solution)/shard_map/all_to_all | solution.py:308
  27.8 0.8 %sum.1 = bf16[16,64,256]{2,1,0:T(8,128)(2,1)} custom-call(bf16[8,2,16,256]{3,2,1,0:T(8,128)(2,1)S(1)} %all_to_all.15.parts_ref, bf16[32,256]{1,0:T(8,128)(2,1)S(1)} %get-tuple-element.10.packed_ref), custom_call_target="tpu_custom_call" | custom-call | tf_op jit(solution)/shard_map/sum/pallas_call | solution.py:309
  28.6 6.8 %all-to-all-start.1 = ((bf16[16,64,256]{2,1,0:T(8,128)(2,1)}), bf16[16,64,256]{2,1,0:T(8,128)(2,1)S(1)}, u32[]{:S(2)}, u32[]{:S(2)}) async-start(bf16[16,64,256]{2,1,0:T(8,128)(2,1)} %sum.1), calls=%async_computation.1 | async-start | bytes 1048576 | tf_op jit(solution)/shard_map/all_to_all | solution.py:317
  35.4 9.3 %all-to-all-done.1.got_ref = bf16[16,64,256]{2,1,0:T(8,128)(2,1)S(1)} async-done(((bf16[16,64,256]{2,1,0:T(8,128)(2,1)}), bf16[16,64,256]{2,1,0:T(8,128)(2,1)S(1)}, u32[]{:S(2)}, u32[]{:S(2)}) %all-to-all-start.1) | async-done | bytes 524320 | tf_op jit(solution)/shard_map/all_to_all | solution.py:317
  44.7 0.0 copy-done.4
  44.7 0.0 copy-done.8
  44.7 0.0 copy-done.9
  44.7 0.0 copy-done.12
  44.7 0.0 copy-done.13
  44.7 1.1 %mix.1 = bf16[8,2,16,256]{3,2,1,0:T(8,128)(2,1)S(1)} custom-call(s32[1]{0:T(128)} %bitcast.2.index_ref, bf16[16,64,256]{2,1,0:T(8,128)(2,1)S(1)} %all-to-all-done.1.got_ref, f32[16,512]{1,0:T(8,128)S(1)} %copy-done.12, f32[16,256]{1,0:T(8,128)S(1)} %copy-done.13, bf16[256,256]{1,0:T(8,128)(2,1)S(1)} %copy-done.9, f32[16,16,32]{2,1,0:T(8,128)S(1)} %copy-done.8, ...), custom_call_target="tpu_custom_call" | custom-call | tf_op jit(solution)/shard_map/mix/pallas_call | solution.py:318
  45.8 11.2 %all_to_all.16.own_ref = bf16[8,2,16,256]{3,2,1,0:T(8,128)(2,1)S(1)} all-to-all(bf16[8,2,16,256]{3,2,1,0:T(8,128)(2,1)S(1)} %mix.1), channel_id=1, replica_groups={{0,2,4,6,8,10,12,14},{1,3,5,7,9,11,13,15},{16,18,20,22,24,26,28,30},{17..., dimensions={0} | all-to-all | bytes 262144 | tf_op jit(solution)/shard_map/all_to_all | solution.py:326
  57.0 3.6 %collective-permute-start.1 = (bf16[8,2,16,256]{3,2,1,0:T(8,128)(2,1)S(1)}, bf16[8,2,16,256]{3,2,1,0:T(8,128)(2,1)S(1)}, u32[]{:S(2)}, u32[]{:S(2)}) collective-permute-start(bf16[8,2,16,256]{3,2,1,0:T(8,128)(2,1)S(1)} %all_to_all.16.own_ref), channel_id=1, source_target_pairs={{0,1},{1,0},{2,3},{3,2},{4,5},{5,4},{6,7},{7,6},{8,9},{9,8},{10,11... | collective-permute-start | bytes 393224 | tf_op jit(solution)/shard_map/ppermute | solution.py:327
  60.6 1.0 %collective-permute-done.1.other_ref = bf16[8,2,16,256]{3,2,1,0:T(8,128)(2,1)S(1)} collective-permute-done((bf16[8,2,16,256]{3,2,1,0:T(8,128)(2,1)S(1)}, bf16[8,2,16,256]{3,2,1,0:T(8,128)(2,1)S(1)}, u32[]{:S(2)}, u32[]{:S(2)}) %collective-permute-start.1) | collective-permute-done | bytes 131104 | tf_op jit(solution)/shard_map/ppermute | solution.py:327
  61.5 0.0 copy-done.2
  61.6 0.0 copy-done.11
  61.6 0.0 copy-start.1
  61.6 2.2 %copy-done.1 = bf16[2,16,16,16,256]{4,3,2,1,0:T(8,128)(2,1)S(1)} copy-done((bf16[2,16,16,16,256]{4,3,2,1,0:T(8,128)(2,1)S(1)}, bf16[2,16,16,16,256]{4,3,2,1,0:T(8,128)(2,1)}, u32[]{:S(2)}) %copy-start.1) | copy-done | bytes 4194328
  63.8 7.4 %inverse.1 = bf16[2,16,16,16,256]{4,3,2,1,0:T(8,128)(2,1)} custom-call(s32[1]{0:T(128)} %bitcast.index_ref, bf16[2,16,16,16,256]{4,3,2,1,0:T(8,128)(2,1)S(1)} %copy-done.1, bf16[16,16]{1,0:T(8,128)(2,1)S(1)} %copy-done.14, f32[1,16]{1,0:T(1,128)S(1)} %bitcast.5, bf16[8,2,16,256]{3,2,1,0:T(8,128)(2,1)S(1)} %all_to_all.16.own_ref, ...), custom_call_target="tpu_custom_call" | custom-call | tf_op jit(solution)/shard_map/inverse/pallas_call | solution.py:328
  (13 shorter events, 0.1 us)
Async XLA Ops:
  0.0 2.2 %copy-start = (bf16[2,16,16,16,256]{4,3,2,1,0:T(8,128)(2,1)S(1)}, bf16[2,16,16,16,256]{4,3,2,1,0:T(8,128)(2,1)}, u32[]{:S(2)}) copy-start(bf16[2,16,16,16,256]{4,3,2,1,0:T(8,128)(2,1)} %field_ref.3) | copy-start | bytes 12582916
  2.2 1.0 %copy-start.3 = (f32[16,16,512]{2,1,0:T(8,128)S(1)}, f32[16,16,512]{2,1,0:T(8,128)}, u32[]{:S(2)}) copy-start(f32[16,16,512]{2,1,0:T(8,128)} %constant.29.clone.table_y_ref) | copy-start | bytes 1572868
  3.2 0.9 %copy-start.5 = (f32[1,1,2,16,16,16]{5,4,3,2,1,0:T(8,128)S(1)}, f32[1,1,2,16,16,16]{5,4,3,2,1,0:T(8,128)}, u32[]{:S(2)}) copy-start(f32[1,1,2,16,16,16]{5,4,3,2,1,0:T(8,128)} %param.15) | copy-start | bytes 98308
  4.2 0.9 %copy-start.6 = (f32[256,256]{1,0:T(8,128)S(1)}, f32[256,256]{1,0:T(8,128)}, u32[]{:S(2)}) copy-start(f32[256,256]{1,0:T(8,128)} %constant.27.clone.table_z_ref) | copy-start | bytes 786436
  5.1 0.7 %copy-start.10 = (f32[16,256]{1,0:T(8,128)S(1)}, f32[16,256]{1,0:T(8,128)}, u32[]{:S(2)}) copy-start(f32[16,256]{1,0:T(8,128)} %constant.28.clone.lanes_x_ref) | copy-start | bytes 49156
  5.8 38.9 %copy-start.4 = (bf16[1024,128]{1,0:T(8,128)(2,1)S(1)}, bf16[1024,128]{1,0:T(8,128)(2,1)}, u32[]{:S(2)}) copy-start(bf16[1024,128]{1,0:T(8,128)(2,1)} %constant.34.clone.spread_ref) | copy-start | bytes 786436
  5.9 38.9 %copy-start.8 = (f32[16,16,32]{2,1,0:T(8,128)S(1)}, f32[16,16,32]{2,1,0:T(8,128)}, u32[]{:S(2)}) copy-start(f32[16,16,32]{2,1,0:T(8,128)} %constant.33.clone.back_x_ref) | copy-start | bytes 98308
  5.9 38.9 %copy-start.9 = (bf16[256,256]{1,0:T(8,128)(2,1)S(1)}, bf16[256,256]{1,0:T(8,128)(2,1)}, u32[]{:S(2)}) copy-start(bf16[256,256]{1,0:T(8,128)(2,1)} %constant.32.clone.fold_ref) | copy-start | bytes 393220
  5.9 38.9 %copy-start.12 = (f32[16,512]{1,0:T(8,128)S(1)}, f32[16,512]{1,0:T(8,128)}, u32[]{:S(2)}) copy-start(f32[16,512]{1,0:T(8,128)} %constant.30.clone.table_x_ref) | copy-start | bytes 98308
  5.9 38.9 %copy-start.13 = (f32[16,256]{1,0:T(8,128)S(1)}, f32[16,256]{1,0:T(8,128)}, u32[]{:S(2)}) copy-start(f32[16,256]{1,0:T(8,128)} %constant.31.clone.lanes_v_ref) | copy-start | bytes 49156
  5.9 55.7 %copy-start.2 = (f32[16,16,512]{2,1,0:T(8,128)S(1)}, f32[16,16,512]{2,1,0:T(8,128)}, u32[]{:S(2)}) copy-start(f32[16,16,512]{2,1,0:T(8,128)} %constant.35.clone.table_y_ref) | copy-start | bytes 1572868
  5.9 55.7 %copy-start.7 = (bf16[256,256]{1,0:T(8,128)(2,1)S(1)}, bf16[256,256]{1,0:T(8,128)(2,1)}, u32[]{:S(2)}) copy-start(bf16[256,256]{1,0:T(8,128)(2,1)} %constant.36.clone.table_z_ref) | copy-start | bytes 393220
  5.9 55.7 %copy-start.11 = (f32[16,256]{1,0:T(8,128)S(1)}, f32[16,256]{1,0:T(8,128)}, u32[]{:S(2)}) copy-start(f32[16,256]{1,0:T(8,128)} %constant.28.clone.lanes_x_ref) | copy-start | bytes 49156
  5.9 55.6 %copy-start.14 = (bf16[16,16]{1,0:T(8,128)(2,1)S(1)}, bf16[16,16]{1,0:T(8,128)(2,1)}, u32[]{:S(2)}) copy-start(bf16[16,16]{1,0:T(8,128)(2,1)} %skip_ref.1) | copy-start | bytes 1540
  5.9 55.6 %copy-start.15 = (f32[16]{0:T(128)S(1)}, f32[16]{0:T(128)}, u32[]{:S(2)}) copy-start(f32[16]{0:T(128)} %param.17) | copy-start | bytes 196
  9.3 4.3 %collective-permute-start = (bf16[8,2,16,256]{3,2,1,0:T(8,128)(2,1)S(1)}, bf16[8,2,16,256]{3,2,1,0:T(8,128)(2,1)S(1)}, u32[]{:S(2)}, u32[]{:S(2)}) collective-permute-start(bf16[8,2,16,256]{3,2,1,0:T(8,128)(2,1)S(1)} %get-tuple-element.9), channel_id=1, source_target_pairs={{0,1},{1,0},{2,3},{3,2},{4,5},{5,4},{6,7},{7,6},{8,9},{9,8},{10,11... | collective-permute-start | bytes 393224 | tf_op jit(solution)/shard_map/ppermute | solution.py:306
  28.6 16.1 %all-to-all-start.1 = ((bf16[16,64,256]{2,1,0:T(8,128)(2,1)}), bf16[16,64,256]{2,1,0:T(8,128)(2,1)S(1)}, u32[]{:S(2)}, u32[]{:S(2)}) async-start(bf16[16,64,256]{2,1,0:T(8,128)(2,1)} %sum.1), calls=%async_computation.1 | async-start | bytes 1048576 | tf_op jit(solution)/shard_map/all_to_all | solution.py:317
  57.0 4.6 %collective-permute-start.1 = (bf16[8,2,16,256]{3,2,1,0:T(8,128)(2,1)S(1)}, bf16[8,2,16,256]{3,2,1,0:T(8,128)(2,1)S(1)}, u32[]{:S(2)}, u32[]{:S(2)}) collective-permute-start(bf16[8,2,16,256]{3,2,1,0:T(8,128)(2,1)S(1)} %all_to_all.16.own_ref), channel_id=1, source_target_pairs={{0,1},{1,0},{2,3},{3,2},{4,5},{5,4},{6,7},{7,6},{8,9},{9,8},{10,11... | collective-permute-start | bytes 393224 | tf_op jit(solution)/shard_map/ppermute | solution.py:327
  61.6 2.2 %copy-start.1 = (bf16[2,16,16,16,256]{4,3,2,1,0:T(8,128)(2,1)S(1)}, bf16[2,16,16,16,256]{4,3,2,1,0:T(8,128)(2,1)}, u32[]{:S(2)}) copy-start(bf16[2,16,16,16,256]{4,3,2,1,0:T(8,128)(2,1)} %field_ref.3) | copy-start | bytes 12582916
where the time goes:
time: 71.6 us; the launch traced here: 71.2 us
  blocking collectives  25.3 us (35%)
  starting transfers between devices  13.7 us (19%)
  Pallas kernels  12.6 us (18%)
  waiting for transfers between devices  11.3 us (16%)
  local copies, waits for them, and re-layouts  8.08 us (11%)
    all_to_all x1, blocking collectives, on_device(): sums = lax.all_to_all(sums, 'py', 0, 0, axis_index_groups=CHIPS, tiled=True)  14.1 us
    all_to_all x1, blocking collectives, on_device(): lax.all_to_all(message, 'py', 0, 0, axis_index_groups=CHIPS, tiled=True)  11.2 us
    all_to_all x1, waiting for transfers between devices, on_device(): message = lax.all_to_all(message, 'px', 0, 0, tiled=True)  9.31 us
    unnamed x32, local copies, waits for them, and re-layouts  8.08 us
    pallas_call x1, Pallas kernels, on_device(): pl.pallas_call(inverse_kernel, name='inverse', in_specs=[SM, ANY, VM, VM,...  7.39 us
    all_to_all x1, starting transfers between devices, on_device(): message = lax.all_to_all(message, 'px', 0, 0, tiled=True)  6.76 us
    ppermute x1, starting transfers between devices, on_device(): other = lax.ppermute(own, 'py', PAIR)  3.58 us
    pallas_call x1, Pallas kernels, on_device(): pl.pallas_call(forward_kernel, name='forward', in_specs=[SM, ANY, VM, VM,...  3.34 us
  transfers between devices with their start and end apart: 3, of which 3 were waited for; matrix products, arithmetic and copies ran while one was open for 0% of the time, Pallas kernels for 0%

commit v1 on v0

--- a/solution.py
+++ b/solution.py
@@ -39,7 +39,12 @@
     depth = np.stack([np.cos(angle), -np.sin(angle)], axis=1)
     forward_z = np.repeat(depth[:, :, None, :], RANK, axis=2).reshape(GRID, LANES)
     w = np.where(kz == 0, 1.0, 2.0) * (0.5 / math.sqrt(MODES**3))
-    inverse_z = np.repeat((depth * w)[:, :, None, :], RANK, axis=2).reshape(GRID, LANES).T
+    inverse_z = np.zeros((4, 4, 2, MODES, GRID))
+    for j in range(4):
+        inverse_z[j, j] = (depth * w).transpose(1, 2, 0)
+    inverse_z[:, :3, 1, 0] = 1.0
+    inverse_z = inverse_z.reshape(4, 128, GRID)
+    expand_x = np.einsum("xr,ab,kl->arkxbl", basis, np.eye(2), np.eye(MODES)).reshape(LANES, 512)
     lanes_x = np.tile(np.repeat(basis, MODES, axis=1), (1, 2))
 
     forward_y = np.zeros((16, 16, 2, 16, 16))
@@ -86,6 +91,7 @@
     return dict(
         forward_z=forward_z.astype(f32),
         inverse_z=inverse_z.astype(f32).astype(bf16),
+        expand_x=expand_x.astype(f32).astype(bf16),
         lanes_x=lanes_x.astype(f32),
         forward_y=forward_y.reshape(16, 16, 512).astype(f32),
         inverse_y=inverse_y.reshape(16, 16, 512).astype(f32),
@@ -128,40 +134,59 @@
 
 
 def forward_kernel(
-    index_ref, field_ref, weight_ref, table_z_ref, lanes_x_ref, table_y_ref,
-    keep_ref, send_ref, packed_ref, held, total, arrived,
+    index_ref, field_hbm, weight_hbm, table_z_hbm, lanes_x_hbm, table_y_hbm,
+    keep_ref, send_ref, packed_ref, held_ref,
+    weight_ref, table_z_ref, lanes_x_ref, table_y_ref, total, arrived, loaded,
 ):
+    small = [
+        pltpu.make_async_copy(source, target, loaded.at[i])
+        for i, (source, target) in enumerate(
+            [
+                (weight_hbm, weight_ref),
+                (table_y_hbm.at[index_ref[0]], table_y_ref),
+                (table_z_hbm, table_z_ref),
+                (lanes_x_hbm, lanes_x_ref),
+            ]
+        )
+    ]
+    for copy in small:
+        copy.start()
+
     def fetch(x):
-        return pltpu.make_async_copy(field_ref.at[:, :, x], held.at[x], arrived.at[x])
+        return pltpu.make_async_copy(field_hbm.at[:, :, x], held_ref.at[x], arrived.at[x])
 
     for x in range(BLOCK):
         fetch(x).start()
 
     place = (iota((MODES, LANES), 0) == iota((MODES, LANES), 1) % MODES).astype(jnp.bfloat16)
+    rows = iota((512, LANES), 0) % 16
+    gather = (iota((32, 512), 0) == iota((32, 512), 1) // 16).astype(jnp.bfloat16)
+    small[0].wait()
     wide = dot(weight_ref[...].astype(jnp.bfloat16), place)
-    rows = iota((512, LANES), 0) % 16
     wide = masked(wide, rows == iota((512, LANES), 1) // MODES)
-    gather = (iota((32, 512), 0) == iota((32, 512), 1) // 16).astype(jnp.bfloat16)
     packed_ref[...] = dot(gather, wide).astype(jnp.bfloat16)
 
     shape = (256, 512)
+    small[1].wait()
     table_y = masked(
-        repeat_rows(table_y_ref[index_ref[0]]), iota(shape, 0) % 16 == iota(shape, 1) % 256 // 16
-    )
+        repeat_rows(table_y_ref[...]), iota(shape, 0) % 16 == iota(shape, 1) % 256 // 16
+    )
+    small[2].wait()
+    small[3].wait()
 
     group = 4
     for start in range(0, BLOCK, group):
-        for x in range(start, start + group):
-            fetch(x).wait()
-        data = jnp.concatenate(
-            [held[x].reshape(SLICES * 256, GRID) for x in range(start, start + group)], axis=1
-        )
         table = jnp.concatenate(
             [
                 (table_z_ref[...] * lanes_x_ref[x : x + 1, :]).astype(jnp.bfloat16)
                 for x in range(start, start + group)
             ],
             axis=0,
+        )
+        for x in range(start, start + group):
+            fetch(x).wait()
+        data = jnp.concatenate(
+            [held_ref[x].reshape(SLICES * 256, GRID) for x in range(start, start + group)], axis=1
         )
         part = dot(data, table)
         total[...] = part if start == 0 else total[...] + part
@@ -224,48 +249,47 @@
 
 
 def inverse_kernel(
-    index_ref, field_ref, skip_ref, bias_ref, own_ref, other_ref, table_y_ref, table_z_ref, lanes_x_ref,
-    out_ref, held, ready, left, bias, modes, arrived, sent,
+    index_ref, held_ref, skip_ref, bias_ref, own_ref, other_ref, table_y_ref, expand_ref, table_z_ref,
+    out_ref, ready, sent,
 ):
-    def fetch(x):
-        return pltpu.make_async_copy(field_ref.at[:, :, x], held.at[x], arrived.at[x])
-
     def store(x):
         return pltpu.make_async_copy(ready.at[x], out_ref.at[:, :, x], sent.at[x])
 
-    for x in range(BLOCK):
-        fetch(x).start()
+    shape = (256, 256)
+    place = (iota((16, 256), 0) == iota((16, 256), 1) // 16).astype(jnp.bfloat16)
+    skip = repeat_rows(dot(skip_ref[...], place))
+    skip = masked(skip, iota(shape, 0) % 16 == iota(shape, 1) % 16)
+    one = iota((256, 16), 0) // 16 == iota((256, 16), 1)
+    bias = jnp.sum(jnp.where(one, bias_ref[...], 0.0), axis=1, keepdims=True)
+    parts = []
+    for _ in range(3):
+        parts.append(bias.astype(jnp.bfloat16).astype(jnp.float32))
+        bias = bias - parts[-1]
 
     shape = (256, 512)
     table_y = masked(
         tile_rows(table_y_ref[index_ref[0]]), iota(shape, 0) // 16 == iota(shape, 1) % 16
     )
+    lane = iota(shape, 1) % 128
+    modes = []
     for b in range(SLICES):
         data = [ref[:, b].reshape(128, LANES) for ref in (own_ref, other_ref)]
         data = jnp.concatenate(data, axis=0).astype(jnp.float32)
-        modes[b] = dot(table_y, with_turned(data))
-
-    shape = (256, 256)
-    place = (iota((16, 256), 0) == iota((16, 256), 1) // 16).astype(jnp.bfloat16)
-    skip = repeat_rows(dot(skip_ref[...], place))
-    left[...] = masked(skip, iota(shape, 0) % 16 == iota(shape, 1) % 16)
-    one = iota((256, 16), 0) // 16 == iota((256, 16), 1)
-    column = jnp.sum(jnp.where(one, bias_ref[...], 0.0), axis=1, keepdims=True)
-    bias[...] = jnp.broadcast_to(column, bias.shape)
-
-    def step(x, carry):
-        fetch(x).wait()
-        lanes = lanes_x_ref[pl.ds(x, 1), :]
+        rows = dot(table_y, with_turned(data)).astype(jnp.bfloat16)
+        rows = dot(rows, expand_ref[...])
+        for j in range(3):
+            rows = jnp.where(lane == 32 * j + 16, parts[j], rows)
+        modes.append(rows.astype(jnp.bfloat16))
+
+    for x in range(BLOCK):
+        at = x // 4 * 128
         for b in range(SLICES):
-            a = jnp.concatenate([left[...], (modes[b] * lanes).astype(jnp.bfloat16)], axis=1)
-            c = jnp.concatenate([held[x, b].reshape(256, GRID), table_z_ref[...]], axis=0)
-            value = dot(a, c) + bias[...]
-            value = 0.5 * value * (1.0 + lax.erf(value * math.sqrt(0.5)))
+            value = dot(modes[b][:, at : at + 128], table_z_ref[x % 4])
+            value = value + dot(skip, held_ref[x, b].reshape(256, GRID))
+            half = 0.5 * value
+            value = half + half * lax.erf(value * math.sqrt(0.5))
             ready[x, b] = value.astype(jnp.bfloat16).reshape(CHANNELS, BLOCK, GRID)
         store(x).start()
-        return carry
-
-    lax.fori_loop(0, BLOCK, step, 0)
     for x in range(BLOCK):
         store(x).wait()
 
@@ -290,19 +314,34 @@
     block = (SLICES, CHANNELS, BLOCK, GRID)
     part = (Z_CHIPS, SLICES, CHANNELS, LANES)
 
-    keep, send, packed = pl.pallas_call(
+    far = [
+        pltpu.with_memory_space_constraint(a, pltpu.HBM)
+        for a in (
+            field, spectral_weight.reshape(512, MODES), t["forward_z"], t["lanes_x"], t["forward_y"],
+        )
+    ]
+    keep, send, packed, held = pl.pallas_call(
         forward_kernel,
         name="forward",
-        in_specs=[SM, ANY, VM, VM, VM, VM],
-        out_specs=[VM, VM, VM],
-        out_shape=[shape_of(part, f32), shape_of(part, bf16), shape_of((32, LANES), bf16)],
+        in_specs=[SM, ANY, ANY, ANY, ANY, ANY],
+        out_specs=[VM, VM, VM, VM],
+        out_shape=[
+            shape_of(part, f32),
+            shape_of(part, bf16),
+            shape_of((32, LANES), bf16),
+            pltpu.VMEM((BLOCK, *block), bf16),
+        ],
         scratch_shapes=[
-            pltpu.VMEM((BLOCK, *block), bf16),
+            pltpu.VMEM((512, MODES), f32),
+            pltpu.VMEM((GRID, LANES), f32),
+            pltpu.VMEM((BLOCK, LANES), f32),
+            pltpu.VMEM((16, 512), f32),
             pltpu.VMEM((512, LANES), f32),
             pltpu.SemaphoreType.DMA((BLOCK,)),
+            pltpu.SemaphoreType.DMA((4,)),
         ],
         compiler_params=PARAMS,
-    )(q, field, spectral_weight.reshape(512, MODES), t["forward_z"], t["lanes_x"], t["forward_y"])
+    )(q, *far)
     got = lax.ppermute(send, "py", PAIR)
     sums = (keep + got.astype(f32)).astype(bf16)
     sums = lax.all_to_all(sums, "py", 0, 0, axis_index_groups=CHIPS, tiled=True)
@@ -328,20 +367,15 @@
     return pl.pallas_call(
         inverse_kernel,
         name="inverse",
-        in_specs=[SM, ANY, VM, VM, VM, VM, VM, VM, VM],
+        in_specs=[SM, VM, VM, VM, VM, VM, VM, VM, VM],
         out_specs=ANY,
         out_shape=shape_of(field.shape, bf16),
         scratch_shapes=[
             pltpu.VMEM((BLOCK, *block), bf16),
-            pltpu.VMEM((BLOCK, *block), bf16),
-            pltpu.VMEM((256, 256), bf16),
-            pltpu.VMEM((256, GRID), f32),
-            pltpu.VMEM((SLICES, 256, LANES), f32),
-            pltpu.SemaphoreType.DMA((BLOCK,)),
             pltpu.SemaphoreType.DMA((BLOCK,)),
         ],
         compiler_params=PARAMS,
-    )(q, field, skip_weight, bias.reshape(1, 16), own, other, t["inverse_y"], t["inverse_z"], t["lanes_x"])
+    )(q, held, skip_weight, bias.reshape(1, 16), own, other, t["inverse_y"], t["expand_x"], t["inverse_z"])
 
 
 def solution(mesh):

time: 71.6 us -> 65.8 us (0.919)
  local copies, waits for them, and re-layouts: 8.08 us -> 4.24 us
  Pallas kernels: 12.6 us -> 10.9 us
    unnamed x32 -> x24, local copies, waits for them, and re-layouts: 8.08 us -> 4.24 us
    pallas_call x2, Pallas kernels: 10.7 us -> 9.04 us  [the longest x1 5.26 us: on_device(): pl.pallas_call(forward_kernel, name='forward', in_specs=[SM, ANY, ANY, AN...]
where the time goes in v1:
time: 65.8 us; the launch traced here: 65.6 us
  blocking collectives  25.3 us (38%)
  starting transfers between devices  13.6 us (21%)
  waiting for transfers between devices  11.3 us (17%)
  Pallas kernels  10.9 us (17%)
  local copies, waits for them, and re-layouts  4.24 us (6%)
    all_to_all x1, blocking collectives, on_device(): sums = lax.all_to_all(sums, 'py', 0, 0, axis_index_groups=CHIPS, tiled=True)  14.2 us
    all_to_all x1, blocking collectives, on_device(): lax.all_to_all(message, 'py', 0, 0, axis_index_groups=CHIPS, tiled=True)  11.2 us
    all_to_all x1, waiting for transfers between devices, on_device(): message = lax.all_to_all(message, 'px', 0, 0, tiled=True)  9.31 us
    all_to_all x1, starting transfers between devices, on_device(): message = lax.all_to_all(message, 'px', 0, 0, tiled=True)  6.76 us
    pallas_call x1, Pallas kernels, on_device(): pl.pallas_call(forward_kernel, name='forward', in_specs=[SM, ANY, ANY, AN...  5.26 us
    unnamed x24, local copies, waits for them, and re-layouts  4.24 us
    pallas_call x1, Pallas kernels, on_device(): pl.pallas_call(inverse_kernel, name='inverse', in_specs=[SM, VM, VM, VM,...  3.77 us
    ppermute x1, starting transfers between devices, on_device(): other = lax.ppermute(own, 'py', PAIR)  3.58 us
  transfers between devices with their start and end apart: 3, of which 3 were waited for; matrix products, arithmetic and copies ran while one was open for 0% of the time, Pallas kernels for 0%

profile of v1, /device:TPU:1, one launch (start us, length us, event | category | flops | bytes accessed | tf_op | source)
XLA Modules:
  0.0 65.6 jit_solution(1040164224047881733)
XLA Ops:
  0.0 0.0 copy-start.9
  0.0 0.0 copy-start.8
  0.0 0.0 copy-start.2
  0.1 0.0 copy-start.3
  0.1 0.0 copy-start.4
  0.1 0.0 copy-start.10
  0.1 0.0 copy-start.11
  0.1 5.3 %forward.1 = (f32[8,2,16,256]{3,2,1,0:T(8,128)S(1)}, bf16[8,2,16,256]{3,2,1,0:T(8,128)(2,1)S(1)}, bf16[32,256]{1,0:T(8,128)(2,1)S(1)}, bf16[16,2,16,16,256]{4,3,2,1,0:T(8,128)(2,1)S(1)}) custom-call(s32[1]{0:T(128)} %bitcast.index_ref, bf16[2,16,16,16,256]{4,3,2,1,0:T(8,128)(2,1)} %field_hbm.1, f32[512,16]{1,0:T(8,128)} %bitcast.5, ...), custom_call_target="tpu_custom_call" | custom-call | tf_op jit(solution)/shard_map/forward/pallas_call | solution.py:323
  5.4 0.0 copy-start
  5.4 2.0 %copy-done = bf16[16,2,16,16,256]{4,3,2,1,0:T(8,128)(2,1)} copy-done((bf16[16,2,16,16,256]{4,3,2,1,0:T(8,128)(2,1)}, bf16[16,2,16,16,256]{4,3,2,1,0:T(8,128)(2,1)S(1)}, u32[]{:S(2)}) %copy-start) | copy-done | bytes 4194328
  7.4 3.2 %collective-permute-start = (bf16[8,2,16,256]{3,2,1,0:T(8,128)(2,1)S(1)}, bf16[8,2,16,256]{3,2,1,0:T(8,128)(2,1)S(1)}, u32[]{:S(2)}, u32[]{:S(2)}) collective-permute-start(bf16[8,2,16,256]{3,2,1,0:T(8,128)(2,1)S(1)} %get-tuple-element.11), channel_id=1, source_target_pairs={{0,1},{1,0},{2,3},{3,2},{4,5},{5,4},{6,7},{7,6},{8,9},{9,8},{10,11... | collective-permute-start | bytes 393224 | tf_op jit(solution)/shard_map/ppermute | solution.py:345
  10.6 1.0 %collective-permute-done = bf16[8,2,16,256]{3,2,1,0:T(8,128)(2,1)S(1)} collective-permute-done((bf16[8,2,16,256]{3,2,1,0:T(8,128)(2,1)S(1)}, bf16[8,2,16,256]{3,2,1,0:T(8,128)(2,1)S(1)}, u32[]{:S(2)}, u32[]{:S(2)}) %collective-permute-start) | collective-permute-done | bytes 131104 | tf_op jit(solution)/shard_map/ppermute | solution.py:345
  11.6 14.2 %all_to_all.15.parts_ref = bf16[8,2,16,256]{3,2,1,0:T(8,128)(2,1)S(1)} all-to-all(bf16[8,2,16,256]{3,2,1,0:T(8,128)(2,1)S(1)} %add_convert_fusion), channel_id=1, replica_groups={{0,2,4,6,8,10,12,14},{1,3,5,7,9,11,13,15},{16,18,20,22,24,26,28,30},{17..., dimensions={0} | all-to-all | bytes 262144 | tf_op jit(solution)/shard_map/all_to_all | solution.py:347
  25.8 0.8 %sum.1 = bf16[16,64,256]{2,1,0:T(8,128)(2,1)} custom-call(bf16[8,2,16,256]{3,2,1,0:T(8,128)(2,1)S(1)} %all_to_all.15.parts_ref, bf16[32,256]{1,0:T(8,128)(2,1)S(1)} %get-tuple-element.12.packed_ref), custom_call_target="tpu_custom_call" | custom-call | tf_op jit(solution)/shard_map/sum/pallas_call | solution.py:348
  26.6 6.8 %all-to-all-start.1 = ((bf16[16,64,256]{2,1,0:T(8,128)(2,1)}), bf16[16,64,256]{2,1,0:T(8,128)(2,1)S(1)}, u32[]{:S(2)}, u32[]{:S(2)}) async-start(bf16[16,64,256]{2,1,0:T(8,128)(2,1)} %sum.1), calls=%async_computation.1 | async-start | bytes 1048576 | tf_op jit(solution)/shard_map/all_to_all | solution.py:356
  33.4 9.3 %all-to-all-done.1.got_ref = bf16[16,64,256]{2,1,0:T(8,128)(2,1)S(1)} async-done(((bf16[16,64,256]{2,1,0:T(8,128)(2,1)}), bf16[16,64,256]{2,1,0:T(8,128)(2,1)S(1)}, u32[]{:S(2)}, u32[]{:S(2)}) %all-to-all-start.1) | async-done | bytes 524320 | tf_op jit(solution)/shard_map/all_to_all | solution.py:356
  42.7 0.0 copy-done.5
  42.7 0.0 copy-done.6
  42.7 0.0 copy-done.7
  42.7 0.0 copy-done.9
  42.7 0.0 copy-done.8
  42.8 1.1 %mix.1 = bf16[8,2,16,256]{3,2,1,0:T(8,128)(2,1)S(1)} custom-call(s32[1]{0:T(128)} %bitcast.3.index_ref, bf16[16,64,256]{2,1,0:T(8,128)(2,1)S(1)} %all-to-all-done.1.got_ref, f32[16,512]{1,0:T(8,128)S(1)} %copy-done.8, f32[16,256]{1,0:T(8,128)S(1)} %copy-done.9, bf16[256,256]{1,0:T(8,128)(2,1)S(1)} %copy-done.7, f32[16,16,32]{2,1,0:T(8,128)S(1)} %copy-done.6, ...), custom_call_target="tpu_custom_call" | custom-call | tf_op jit(solution)/shard_map/mix/pallas_call | solution.py:357
  43.8 11.2 %all_to_all.16.own_ref = bf16[8,2,16,256]{3,2,1,0:T(8,128)(2,1)S(1)} all-to-all(bf16[8,2,16,256]{3,2,1,0:T(8,128)(2,1)S(1)} %mix.1), channel_id=1, replica_groups={{0,2,4,6,8,10,12,14},{1,3,5,7,9,11,13,15},{16,18,20,22,24,26,28,30},{17..., dimensions={0} | all-to-all | bytes 262144 | tf_op jit(solution)/shard_map/all_to_all | solution.py:365
  55.0 3.6 %collective-permute-start.1 = (bf16[8,2,16,256]{3,2,1,0:T(8,128)(2,1)S(1)}, bf16[8,2,16,256]{3,2,1,0:T(8,128)(2,1)S(1)}, u32[]{:S(2)}, u32[]{:S(2)}) collective-permute-start(bf16[8,2,16,256]{3,2,1,0:T(8,128)(2,1)S(1)} %all_to_all.16.own_ref), channel_id=1, source_target_pairs={{0,1},{1,0},{2,3},{3,2},{4,5},{5,4},{6,7},{7,6},{8,9},{9,8},{10,11... | collective-permute-start | bytes 393224 | tf_op jit(solution)/shard_map/ppermute | solution.py:366
  58.6 1.0 %collective-permute-done.1.other_ref = bf16[8,2,16,256]{3,2,1,0:T(8,128)(2,1)S(1)} collective-permute-done((bf16[8,2,16,256]{3,2,1,0:T(8,128)(2,1)S(1)}, bf16[8,2,16,256]{3,2,1,0:T(8,128)(2,1)S(1)}, u32[]{:S(2)}, u32[]{:S(2)}) %collective-permute-start.1) | collective-permute-done | bytes 131104 | tf_op jit(solution)/shard_map/ppermute | solution.py:366
  59.6 0.0 copy-done.2
  59.6 0.0 copy-done.3
  59.6 0.0 copy-done.4
  59.6 0.0 copy-done.10
  59.6 0.0 copy-start.1
  59.6 2.2 %copy-done.1 = bf16[16,2,16,16,256]{4,3,2,1,0:T(8,128)(2,1)S(1)} copy-done((bf16[16,2,16,16,256]{4,3,2,1,0:T(8,128)(2,1)S(1)}, bf16[16,2,16,16,256]{4,3,2,1,0:T(8,128)(2,1)}, u32[]{:S(2)}) %copy-start.1) | copy-done | bytes 4194328
  61.8 3.8 %inverse.1 = bf16[2,16,16,16,256]{4,3,2,1,0:T(8,128)(2,1)} custom-call(s32[1]{0:T(128)} %bitcast.index_ref, bf16[16,2,16,16,256]{4,3,2,1,0:T(8,128)(2,1)S(1)} %copy-done.1, bf16[16,16]{1,0:T(8,128)(2,1)S(1)} %copy-done.10, f32[1,16]{1,0:T(1,128)S(1)} %bitcast.4, bf16[8,2,16,256]{3,2,1,0:T(8,128)(2,1)S(1)} %all_to_all.16.own_ref, ...), custom_call_target="tpu_custom_call" | custom-call | tf_op jit(solution)/shard_map/inverse/pallas_call | solution.py:367
  (5 shorter events, 0.0 us)
Async XLA Ops:
  0.0 42.7 %copy-start.5 = (bf16[1024,128]{1,0:T(8,128)(2,1)S(1)}, bf16[1024,128]{1,0:T(8,128)(2,1)}, u32[]{:S(2)}) copy-start(bf16[1024,128]{1,0:T(8,128)(2,1)} %constant.36.clone.spread_ref) | copy-start | bytes 786436
  0.0 42.7 %copy-start.6 = (f32[16,16,32]{2,1,0:T(8,128)S(1)}, f32[16,16,32]{2,1,0:T(8,128)}, u32[]{:S(2)}) copy-start(f32[16,16,32]{2,1,0:T(8,128)} %constant.35.clone.back_x_ref) | copy-start | bytes 98308
  0.0 42.7 %copy-start.7 = (bf16[256,256]{1,0:T(8,128)(2,1)S(1)}, bf16[256,256]{1,0:T(8,128)(2,1)}, u32[]{:S(2)}) copy-start(bf16[256,256]{1,0:T(8,128)(2,1)} %constant.34.clone.fold_ref) | copy-start | bytes 393220
  0.0 42.7 %copy-start.9 = (f32[16,256]{1,0:T(8,128)S(1)}, f32[16,256]{1,0:T(8,128)}, u32[]{:S(2)}) copy-start(f32[16,256]{1,0:T(8,128)} %constant.33.clone.lanes_v_ref) | copy-start | bytes 49156
  0.0 42.7 %copy-start.8 = (f32[16,512]{1,0:T(8,128)S(1)}, f32[16,512]{1,0:T(8,128)}, u32[]{:S(2)}) copy-start(f32[16,512]{1,0:T(8,128)} %constant.32.clone.table_x_ref) | copy-start | bytes 98308
  0.0 59.5 %copy-start.2 = (f32[16,16,512]{2,1,0:T(8,128)S(1)}, f32[16,16,512]{2,1,0:T(8,128)}, u32[]{:S(2)}) copy-start(f32[16,16,512]{2,1,0:T(8,128)} %constant.37.clone.table_y_ref) | copy-start | bytes 1572868
  0.1 59.5 %copy-start.3 = (bf16[4,128,256]{2,1,0:T(8,128)(2,1)S(1)}, bf16[4,128,256]{2,1,0:T(8,128)(2,1)}, u32[]{:S(2)}) copy-start(bf16[4,128,256]{2,1,0:T(8,128)(2,1)} %constant.39.clone.table_z_ref) | copy-start | bytes 786436
  0.1 59.5 %copy-start.4 = (bf16[256,512]{1,0:T(8,128)(2,1)S(1)}, bf16[256,512]{1,0:T(8,128)(2,1)}, u32[]{:S(2)}) copy-start(bf16[256,512]{1,0:T(8,128)(2,1)} %constant.38.clone.expand_ref) | copy-start | bytes 786436
  0.1 59.5 %copy-start.10 = (bf16[16,16]{1,0:T(8,128)(2,1)S(1)}, bf16[16,16]{1,0:T(8,128)(2,1)}, u32[]{:S(2)}) copy-start(bf16[16,16]{1,0:T(8,128)(2,1)} %skip_ref.1) | copy-start | bytes 1540
  0.1 59.5 %copy-start.11 = (f32[16]{0:T(128)S(1)}, f32[16]{0:T(128)}, u32[]{:S(2)}) copy-start(f32[16]{0:T(128)} %param.18) | copy-start | bytes 196
  5.4 2.0 %copy-start = (bf16[16,2,16,16,256]{4,3,2,1,0:T(8,128)(2,1)}, bf16[16,2,16,16,256]{4,3,2,1,0:T(8,128)(2,1)S(1)}, u32[]{:S(2)}) copy-start(bf16[16,2,16,16,256]{4,3,2,1,0:T(8,128)(2,1)S(1)} %get-tuple-element.9.held_ref) | copy-start | bytes 12582916
  7.4 4.2 %collective-permute-start = (bf16[8,2,16,256]{3,2,1,0:T(8,128)(2,1)S(1)}, bf16[8,2,16,256]{3,2,1,0:T(8,128)(2,1)S(1)}, u32[]{:S(2)}, u32[]{:S(2)}) collective-permute-start(bf16[8,2,16,256]{3,2,1,0:T(8,128)(2,1)S(1)} %get-tuple-element.11), channel_id=1, source_target_pairs={{0,1},{1,0},{2,3},{3,2},{4,5},{5,4},{6,7},{7,6},{8,9},{9,8},{10,11... | collective-permute-start | bytes 393224 | tf_op jit(solution)/shard_map/ppermute | solution.py:345
  26.6 16.1 %all-to-all-start.1 = ((bf16[16,64,256]{2,1,0:T(8,128)(2,1)}), bf16[16,64,256]{2,1,0:T(8,128)(2,1)S(1)}, u32[]{:S(2)}, u32[]{:S(2)}) async-start(bf16[16,64,256]{2,1,0:T(8,128)(2,1)} %sum.1), calls=%async_computation.1 | async-start | bytes 1048576 | tf_op jit(solution)/shard_map/all_to_all | solution.py:356
  55.0 4.6 %collective-permute-start.1 = (bf16[8,2,16,256]{3,2,1,0:T(8,128)(2,1)S(1)}, bf16[8,2,16,256]{3,2,1,0:T(8,128)(2,1)S(1)}, u32[]{:S(2)}, u32[]{:S(2)}) collective-permute-start(bf16[8,2,16,256]{3,2,1,0:T(8,128)(2,1)S(1)} %all_to_all.16.own_ref), channel_id=1, source_target_pairs={{0,1},{1,0},{2,3},{3,2},{4,5},{5,4},{6,7},{7,6},{8,9},{9,8},{10,11... | collective-permute-start | bytes 393224 | tf_op jit(solution)/shard_map/ppermute | solution.py:366
  59.6 2.2 %copy-start.1 = (bf16[16,2,16,16,256]{4,3,2,1,0:T(8,128)(2,1)S(1)}, bf16[16,2,16,16,256]{4,3,2,1,0:T(8,128)(2,1)}, u32[]{:S(2)}) copy-start(bf16[16,2,16,16,256]{4,3,2,1,0:T(8,128)(2,1)} %copy-done) | copy-start | bytes 12582916

commit v2 on v1

v2 whole, which is shorter than its diff:
```python
import math

import jax
import jax.numpy as jnp
import numpy as np
from jax import lax
from jax.experimental import pallas as pl
from jax.experimental.pallas import tpu as pltpu
from jax.sharding import PartitionSpec as P

GRID = 256
CHANNELS = 16
MODES = 16
SLICES = 2
BLOCK = 16
RANK = 8
EVEN = RANK // 2
HALF = RANK * MODES
LANES = 2 * HALF
Z_CHIPS = 8
GROUP = 4
GROUPS = BLOCK // GROUP
AHEAD = 3
VMEM = 24 * 1024 * 1024
CENTRE = (BLOCK - 1) / 2


def make_tables():
    freq = np.concatenate([np.arange(8), np.arange(-8, 0)]).astype(np.float64)
    turn = 2.0 * np.pi / GRID
    u = np.arange(BLOCK) - CENTRE
    basis, weight = [], []
    for part in (np.cos(np.outer(u, turn * freq)), np.sin(np.outer(u, turn * freq))):
        left, scale, right = np.linalg.svd(part)
        basis.append(left[:, :EVEN])
        weight.append(scale[:EVEN, None] * right[:EVEN])
    basis = np.concatenate(basis, axis=1)
    weight = np.concatenate(weight, axis=0)
    odd = np.arange(RANK) >= EVEN

    kz, z = np.arange(MODES), np.arange(GRID)
    angle = turn * np.outer(z, kz)
    depth = np.stack([np.cos(angle), -np.sin(angle)], axis=1)
    forward_z = np.repeat(depth[:, :, None, :], RANK, axis=2).reshape(GRID, LANES)
    w = np.where(kz == 0, 1.0, 2.0) * (0.5 / math.sqrt(MODES**3))
    inverse_z = (depth * w).transpose(1, 2, 0).reshape(2 * MODES, GRID)
    expand_x = np.einsum("xr,ab->arxb", basis, np.eye(2)).reshape(16, 32)
    expand_x = np.repeat(expand_x, MODES, axis=1)
    lanes_x = np.tile(np.repeat(basis, MODES, axis=1), (1, 2))

    forward_y = np.zeros((16, 16, 2, 16, 16))
    inverse_y = np.zeros((16, 16, 2, 16, 16))
    scale = float(GRID) ** -1.5
    for q in range(16):
        for s in range(2):
            for chip in range(Z_CHIPS):
                theta = turn * freq[2 * chip + ((q % 2) ^ s)] * (16 * q + np.arange(16))
                row = s * Z_CHIPS + chip
                forward_y[q, row, 0] = (np.cos(theta) * scale)[None, :]
                forward_y[q, row, 1] = (np.sin(theta) * scale)[None, :]
                inverse_y[q, :, 0, row] = np.cos(theta)[:, None]
                inverse_y[q, :, 1, row] = -np.sin(theta)[:, None]

    phase = turn * np.outer(freq, 16 * np.arange(16) + CENTRE)
    forward_x = np.stack([np.cos(phase), np.sin(phase)], axis=1)
    forward_x = np.repeat(forward_x[..., None], CHANNELS, axis=3).reshape(16, 512)
    lanes_v = np.tile(np.repeat(weight.T, MODES, axis=1), (1, 2))
    inverse_x = np.zeros((16, 2, RANK, 2, MODES))
    for p in range(16):
        cos, sin = np.cos(phase[:, p]) * weight, np.sin(phase[:, p]) * weight
        real, imag = np.stack([cos, -sin], axis=1), np.stack([sin, cos], axis=1)
        turned = odd[:, None, None]
        inverse_x[p, 0] = np.where(turned, -imag, real)
        inverse_x[p, 1] = np.where(turned, real, imag)
    inverse_x = inverse_x.reshape(16, 16, 32)

    tables = dict(
        forward_z=forward_z,
        inverse_z=inverse_z,
        expand_x=expand_x,
        lanes_x=lanes_x,
        forward_y=forward_y.reshape(16, 16, 512),
        inverse_y=inverse_y.reshape(16, 16, 512),
        forward_x=forward_x,
        lanes_v=lanes_v,
        inverse_x=inverse_x,
    )
    return {name: table.astype(np.float32) for name, table in tables.items()}


def iota(shape, dim):
    return lax.broadcasted_iota(jnp.int32, shape, dim)


def dot(a, b):
    return jnp.dot(a, b, preferred_element_type=jnp.float32)


def repeat_rows(table):
    rows, lanes = table.shape
    return jnp.broadcast_to(table[:, None, :], (rows, 16, lanes)).reshape(rows * 16, lanes)


def tile_rows(table):
    rows, lanes = table.shape
    return jnp.broadcast_to(table[None], (16, rows, lanes)).reshape(rows * 16, lanes)


def masked(table, keep):
    return jnp.where(keep, table, 0.0).astype(jnp.bfloat16)


def turned(data):
    return jnp.concatenate([data[:, HALF:], -data[:, :HALF]], axis=1)


def with_turned(data):
    return jnp.concatenate([data, turned(data)], axis=0).astype(jnp.bfloat16)


def forward_kernel(
    index_ref, field_hbm, weight_hbm, table_z_hbm, lanes_x_hbm, table_y_hbm, back_y_hbm, back_x_hbm,
    keep_ref, send_ref, packed_ref, back_y_ref, back_x_ref, first_ref, second_ref,
    rest, weight_ref, table_z_ref, lanes_x_ref, table_y_ref, total, arrived, loaded,
):
    small = [
        pltpu.make_async_copy(source, target, loaded.at[i])
        for i, (source, target) in enumerate(
            [
                (weight_hbm, weight_ref),
                (table_y_hbm.at[index_ref[1]], table_y_ref),
                (table_z_hbm, table_z_ref),
                (lanes_x_hbm, lanes_x_ref),
                (back_y_hbm.at[index_ref[1]], back_y_ref),
                (back_x_hbm.at[index_ref[0]], back_x_ref),
            ]
        )
    ]
    for copy in small:
        copy.start()
    held = [first_ref, second_ref, rest.at[0], rest.at[1]]

    def fetch(g):
        return pltpu.make_async_copy(field_hbm.at[:, :, pl.ds(g * GROUP, GROUP)], held[g], arrived.at[g])

    for g in range(AHEAD):
        fetch(g).start()

    place = (iota((MODES, LANES), 0) == iota((MODES, LANES), 1) % MODES).astype(jnp.bfloat16)
    rows = iota((512, LANES), 0) % 16
    gather = (iota((32, 512), 0) == iota((32, 512), 1) // 16).astype(jnp.bfloat16)
    small[0].wait()
    wide = dot(weight_ref[...].astype(jnp.bfloat16), place)
    wide = masked(wide, rows == iota((512, LANES), 1) // MODES)
    packed_ref[...] = dot(gather, wide).astype(jnp.bfloat16)

    shape = (256, 512)
    small[1].wait()
    table_y = masked(
        repeat_rows(table_y_ref[...]), iota(shape, 0) % 16 == iota(shape, 1) % 256 // 16
    )
    for copy in small[2:]:
        copy.wait()

    for g in range(GROUPS):
        table = jnp.concatenate(
            [
                (table_z_ref[...] * lanes_x_ref[x : x + 1, :]).astype(jnp.bfloat16)
                for x in range(g * GROUP, (g + 1) * GROUP)
            ],
            axis=0,
        )
        fetch(g).wait()
        if g + AHEAD < GROUPS:
            fetch(g + AHEAD).start()
        data = jnp.concatenate(
            [held[g][:, :, j].reshape(SLICES * 256, GRID) for j in range(GROUP)], axis=1
        )
        part = dot(data, table)
        total[...] = part if g == 0 else total[...] + part

    for b in range(SLICES):
        sums = dot(table_y, with_turned(total[b * 256 : (b + 1) * 256, :]))
        sums = sums.reshape(2, Z_CHIPS, CHANNELS, LANES)
        keep_ref[:, b] = sums[0]
        send_ref[:, b] = sums[1].astype(jnp.bfloat16)


def sum_kernel(parts_ref, packed_ref, out_ref):
    parts = parts_ref[...].astype(jnp.float32)
    sums = jnp.sum(parts, axis=0).reshape(32, LANES).astype(jnp.bfloat16)
    message = jnp.concatenate([sums, packed_ref[...]], axis=0)
    out_ref[...] = jnp.broadcast_to(message[None], out_ref.shape)


def mix_kernel(got_ref, table_x_ref, lanes_v_ref, back_x_ref, out_ref):
    shape = (LANES, LANES)
    row, lane = iota(shape, 0), iota(shape, 1)
    kind = jnp.where(row % HALF // MODES < EVEN, 0, 1)
    step = jnp.where(row < HALF, 0, 1) - jnp.where(lane < HALF, 0, 1)
    fold = jnp.where(kind == 0, jnp.where(step == 0, 1.0, 0.0), step.astype(jnp.float32))
    fold = masked(fold, row % MODES == lane % MODES)
    shape = (RANK * 128, 128)
    row, lane = iota(shape, 0), iota(shape, 1)
    spread = masked(jnp.where(row // 128 == lane // MODES, 1.0, 0.0), row % MODES == lane % MODES)

    shape = (256, 512)
    table_x = masked(repeat_rows(table_x_ref[...]), iota(shape, 0) % 16 == iota(shape, 1) % 16)
    scale = repeat_rows(lanes_v_ref[...])
    mixed = []
    for b in range(SLICES):
        data = got_ref[:, b * 16 : (b + 1) * 16, :].reshape(256, LANES).astype(jnp.float32)
        modes = dot(table_x, with_turned(data)) * scale
        modes = dot(modes.astype(jnp.bfloat16), fold).reshape(MODES, CHANNELS, LANES)
        real, imag = modes[..., :HALF], modes[..., HALF:]
        for h in range(2):
            lanes = slice(h * HALF, (h + 1) * HALF)
            w_real = got_ref[:, 32:48, lanes].astype(jnp.float32)
            w_imag = got_ref[:, 48:64, lanes].astype(jnp.float32)
            out_real = jnp.sum(real * w_real - imag * w_imag, axis=1)
            out_imag = jnp.sum(real * w_imag + imag * w_real, axis=1)
            mixed.append(jnp.concatenate([out_real, out_imag], axis=0))
    mixed = jnp.concatenate(mixed, axis=1)
    mixed = mixed.astype(jnp.bfloat16).astype(jnp.float32)
    back = jnp.dot(
        back_x_ref[...], mixed, precision=lax.Precision.HIGHEST, preferred_element_type=jnp.float32
    )
    own = iota((8, 128), 0) == iota((8, 128), 1) // MODES
    rows = []
    for b in range(SLICES):
        for h in range(2):
            at = (2 * b + h) * 128
            for a in range(2):
                pieces = [
                    jnp.where(own, back[a * RANK + r : a * RANK + r + 1, at : at + 128], 0.0)
                    for r in range(RANK)
                ]
                rows.append(jnp.concatenate(pieces, axis=1))
    rows = jnp.concatenate(rows, axis=0).astype(jnp.bfloat16)
    rows = dot(rows, spread).reshape(SLICES, 2, 2, 8, HALF)
    for b in range(SLICES):
        half = [jnp.concatenate([rows[b, 0, a], rows[b, 1, a]], axis=0) for a in range(2)]
        message = jnp.concatenate(half, axis=1).astype(jnp.bfloat16)
        out_ref[:, b] = jnp.broadcast_to(message[None], (Z_CHIPS, CHANNELS, LANES))


def inverse_kernel(
    field_hbm, first_ref, second_ref, skip_ref, bias_ref, own_ref, other_ref,
    table_y_ref, expand_ref, table_z_ref,
    out_ref, rest, ready, arrived, sent,
):
    held = [first_ref, second_ref, rest.at[0], rest.at[1]]

    def fetch(g):
        return pltpu.make_async_copy(field_hbm.at[:, :, pl.ds(g * GROUP, GROUP)], held[g], arrived.at[g - 2])

    def store(g):
        return pltpu.make_async_copy(ready.at[g], out_ref.at[:, :, pl.ds(g * GROUP, GROUP)], sent.at[g])

    for g in (2, 3):
        fetch(g).start()

    shape = (256, 256)
    place = (iota((16, 256), 0) == iota((16, 256), 1) // 16).astype(jnp.bfloat16)
    skip = repeat_rows(dot(skip_ref[...], place))
    skip = masked(skip, iota(shape, 0) % 16 == iota(shape, 1) % 16)
    one = iota((256, 16), 0) // 16 == iota((256, 16), 1)
    bias = jnp.sum(jnp.where(one, bias_ref[...], 0.0), axis=1, keepdims=True)
    parts = []
    for _ in range(3):
        parts.append(bias.astype(jnp.bfloat16).astype(jnp.float32))
        bias = bias - parts[-1]

    shape = (2 * MODES, GRID)
    ones = jnp.where(iota(shape, 0) == MODES, 1.0, 0.0)
    tables_z = []
    for j in range(GROUP):
        blocks = [ones, ones, ones, jnp.zeros(shape, jnp.float32)]
        blocks[j] = blocks[j] + table_z_ref[...]
        tables_z.append(jnp.concatenate(blocks, axis=0).astype(jnp.bfloat16))

    shape = (256, 512)
    table_y = masked(tile_rows(table_y_ref[...]), iota(shape, 0) // 16 == iota(shape, 1) % 16)
    expand = masked(repeat_rows(expand_ref[...]), iota(shape, 0) % 16 == iota(shape, 1) % 16)
    lane = iota(shape, 1) % 128
    modes = []
    for b in range(SLICES):
        data = [ref[:, b].reshape(128, LANES) for ref in (own_ref, other_ref)]
        data = jnp.concatenate(data, axis=0).astype(jnp.float32)
        rows = dot(table_y, with_turned(data)).astype(jnp.bfloat16)
        rows = dot(rows, expand)
        for j in range(3):
            rows = jnp.where(lane == 32 * j + 16, parts[j], rows)
        modes.append(rows.astype(jnp.bfloat16))

    for g in range(GROUPS):
        if g >= 2:
            fetch(g).wait()
        for j in range(GROUP):
            for b in range(SLICES):
                value = dot(modes[b][:, g * 128 : (g + 1) * 128], tables_z[j])
                value = value + dot(skip, held[g][b, :, j].reshape(256, GRID))
                half = 0.5 * value
                value = half + half * lax.erf(value * math.sqrt(0.5))
                ready[g, b, :, j] = value.astype(jnp.bfloat16).reshape(CHANNELS, BLOCK, GRID)
        store(g).start()
    for g in range(GROUPS):
        store(g).wait()


VM = pl.BlockSpec(memory_space=pltpu.VMEM)
SM = pl.BlockSpec(memory_space=pltpu.SMEM)
ANY = pl.BlockSpec(memory_space=pl.ANY)
PARAMS = pltpu.CompilerParams(vmem_limit_bytes=VMEM)
PAIR = [(i, i ^ 1) for i in range(16)]
CHIPS = [list(range(0, 16, 2)), list(range(1, 16, 2))]


def shape_of(shape, dtype):
    return jax.ShapeDtypeStruct(shape, dtype)


def on_device(field, spectral_weight, skip_weight, bias):
    t = make_tables()
    f32, bf16 = jnp.float32, jnp.bfloat16
    place = jnp.stack([lax.axis_index("px"), lax.axis_index("py")]).astype(jnp.int32)
    planes = (SLICES, CHANNELS, GROUP, BLOCK, GRID)
    part = (Z_CHIPS, SLICES, CHANNELS, LANES)

    far = [
        pltpu.with_memory_space_constraint(a, pltpu.HBM)
        for a in (
            field, spectral_weight.reshape(512, MODES), t["forward_z"], t["lanes_x"], t["forward_y"],
            t["inverse_y"], t["inverse_x"],
        )
    ]
    keep, send, packed, back_y, back_x, *held = pl.pallas_call(
        forward_kernel,
        name="forward",
        in_specs=[SM] + [ANY] * 7,
        out_specs=[VM] * 7,
        out_shape=[
            shape_of(part, f32),
            shape_of(part, bf16),
            shape_of((32, LANES), bf16),
            shape_of((16, 512), f32),
            shape_of((16, 32), f32),
            pltpu.VMEM(planes, bf16),
            pltpu.VMEM(planes, bf16),
        ],
        scratch_shapes=[
            pltpu.VMEM((2, *planes), bf16),
            pltpu.VMEM((512, MODES), f32),
            pltpu.VMEM((GRID, LANES), f32),
            pltpu.VMEM((BLOCK, LANES), f32),
            pltpu.VMEM((16, 512), f32),
            pltpu.VMEM((512, LANES), f32),
            pltpu.SemaphoreType.DMA((GROUPS,)),
            pltpu.SemaphoreType.DMA((6,)),
        ],
        compiler_params=PARAMS,
    )(place, *far)
    got = lax.ppermute(send, "py", PAIR)
    sums = (keep + got.astype(f32)).astype(bf16)
    sums = lax.all_to_all(sums, "py", 0, 0, axis_index_groups=CHIPS, tiled=True)
    message = pl.pallas_call(
        sum_kernel,
        name="sum",
        in_specs=[VM, VM],
        out_specs=VM,
        out_shape=shape_of((16, 64, LANES), bf16),
        compiler_params=PARAMS,
    )(sums, packed)
    message = lax.all_to_all(message, "px", 0, 0, tiled=True)
    message = pl.pallas_call(
        mix_kernel,
        name="mix",
        in_specs=[VM, VM, VM, VM],
        out_specs=VM,
        out_shape=shape_of(part, bf16),
        compiler_params=PARAMS,
    )(message, t["forward_x"], t["lanes_v"], back_x)
    own = lax.all_to_all(message, "py", 0, 0, axis_index_groups=CHIPS, tiled=True)
    other = lax.ppermute(own, "py", PAIR)
    return pl.pallas_call(
        inverse_kernel,
        name="inverse",
        in_specs=[ANY] + [VM] * 9,
        out_specs=ANY,
        out_shape=shape_of(field.shape, bf16),
        scratch_shapes=[
            pltpu.VMEM((2, *planes), bf16),
            pltpu.VMEM((GROUPS, *planes), bf16),
            pltpu.SemaphoreType.DMA((2,)),
            pltpu.SemaphoreType.DMA((GROUPS,)),
        ],
        compiler_params=PARAMS,
    )(far[0], *held, skip_weight, bias.reshape(1, 16), own, other, back_y, t["expand_x"], t["inverse_z"])


def solution(mesh):
    return jax.shard_map(
        on_device,
        mesh=mesh,
        in_specs=(P(None, None, "px", "py", None), P("px", "py", None, None, None, None), P(), P()),
        out_specs=P(None, None, "px", "py", None),
        check_vma=False,
    )
```

time: 65.8 us -> 60.9 us (0.926)
  blocking collectives: 25.3 us -> 41.2 us
  waiting for transfers between devices: 11.3 us -> 1.97 us
  starting transfers between devices: 13.6 us -> 6.92 us
  local copies, waits for them, and re-layouts: 4.24 us -> 0.03 us
    all_to_all x0 -> x1, blocking collectives: none -> 15.9 us  [on_device(): message = lax.all_to_all(message, 'px', 0, 0, tiled=True)]
    all_to_all x1 -> x0, waiting for transfers between devices: 9.31 us -> none  [on_device(): message = lax.all_to_all(message, 'px', 0, 0, tiled=True)]
    all_to_all x1 -> x0, starting transfers between devices: 6.76 us -> none  [on_device(): message = lax.all_to_all(message, 'px', 0, 0, tiled=True)]
    unnamed x24 -> x12, local copies, waits for them, and re-layouts: 4.24 us -> 0.03 us
    pallas_call x1, Pallas kernels: 0.85 us -> 0.04 us  [on_device(): pl.pallas_call(sum_kernel, name='sum', in_specs=[VM, VM], out_specs=VM, o...]
  transfers between devices with their start and end apart: 3 -> 2, of which waited for: 3 -> 2; matrix products, arithmetic and copies ran while one was open for 0% -> 0% of each run, Pallas kernels for 0% -> 0%
where the time goes in v2:
time: 60.9 us; the launch traced here: 60.7 us
  blocking collectives  41.2 us (68%)
  Pallas kernels  10.5 us (17%)
  starting transfers between devices  6.92 us (11%)
  waiting for transfers between devices  1.97 us (3%)
    all_to_all x1, blocking collectives, on_device(): message = lax.all_to_all(message, 'px', 0, 0, tiled=True)  15.9 us
    all_to_all x1, blocking collectives, on_device(): sums = lax.all_to_all(sums, 'py', 0, 0, axis_index_groups=CHIPS, tiled=True)  14.1 us
    all_to_all x1, blocking collectives, on_device(): lax.all_to_all(message, 'py', 0, 0, axis_index_groups=CHIPS, tiled=True)  11.2 us
    pallas_call x1, Pallas kernels, on_device(): pl.pallas_call(forward_kernel, name='forward', in_specs=[SM] + [ANY] * 7,...  4.83 us
    pallas_call x1, Pallas kernels, on_device(): pl.pallas_call(inverse_kernel, name='inverse', in_specs=[ANY] + [VM] * 9,...  4.55 us
    ppermute x1, starting transfers between devices, on_device(): other = lax.ppermute(own, 'py', PAIR)  3.58 us
    ppermute x1, starting transfers between devices, on_device(): got = lax.ppermute(send, 'py', PAIR)  3.35 us
  transfers between devices with their start and end apart: 2, of which 2 were waited for; matrix products, arithmetic and copies ran while one was open for 0% of the time, Pallas kernels for 0%

profile of v2, /device:TPU:1, one launch (start us, length us, event | category | flops | bytes accessed | tf_op | source)
XLA Modules:
  0.0 60.7 jit_solution(6301433603221433691)
XLA Ops:
  0.0 0.1 pad_add_fusion.index_ref
  0.1 0.0 copy-start.2
  0.1 0.0 copy-start.3
  0.1 0.0 copy-start
  0.1 0.0 copy-start.1
  0.1 0.0 copy-start.4
  0.1 0.0 copy-start.5
  0.1 4.8 %forward.1 = (f32[8,2,16,256]{3,2,1,0:T(8,128)S(1)}, bf16[8,2,16,256]{3,2,1,0:T(8,128)(2,1)S(1)}, bf16[32,256]{1,0:T(8,128)(2,1)S(1)}, f32[16,512]{1,0:T(8,128)S...) custom-call(s32[2]{0:T(128)S(1)} %pad_add_fusion.index_ref, ...), custom_call_target="tpu_custom_call" | custom-call | tf_op jit(solution)/shard_map/forward/pallas_call | solution.py:337
  4.9 3.3 %collective-permute-start = (bf16[8,2,16,256]{3,2,1,0:T(8,128)(2,1)S(1)}, bf16[8,2,16,256]{3,2,1,0:T(8,128)(2,1)S(1)}, u32[]{:S(2)}, u32[]{:S(2)}) collective-permute-start(bf16[8,2,16,256]{3,2,1,0:T(8,128)(2,1)S(1)} %get-tuple-element.15), channel_id=1, source_target_pairs={{0,1},{1,0},{2,3},{3,2},{4,5},{5,4},{6,7},{7,6},{8,9},{9,8},{10,11... | collective-permute-start | bytes 393224 | tf_op jit(solution)/shard_map/ppermute | solution.py:363
  8.3 1.0 %collective-permute-done = bf16[8,2,16,256]{3,2,1,0:T(8,128)(2,1)S(1)} collective-permute-done((bf16[8,2,16,256]{3,2,1,0:T(8,128)(2,1)S(1)}, bf16[8,2,16,256]{3,2,1,0:T(8,128)(2,1)S(1)}, u32[]{:S(2)}, u32[]{:S(2)}) %collective-permute-start) | collective-permute-done | bytes 131104 | tf_op jit(solution)/shard_map/ppermute | solution.py:363
  9.3 14.1 %all_to_all.15.parts_ref = bf16[8,2,16,256]{3,2,1,0:T(8,128)(2,1)S(1)} all-to-all(bf16[8,2,16,256]{3,2,1,0:T(8,128)(2,1)S(1)} %add_convert_fusion), channel_id=1, replica_groups={{0,2,4,6,8,10,12,14},{1,3,5,7,9,11,13,15},{16,18,20,22,24,26,28,30},{17..., dimensions={0} | all-to-all | bytes 262144 | tf_op jit(solution)/shard_map/all_to_all | solution.py:365
  23.5 15.9 %all_to_all.16.got_ref = bf16[16,64,256]{2,1,0:T(8,128)(2,1)S(1)} all-to-all(bf16[16,64,256]{2,1,0:T(8,128)(2,1)S(1)} %sum.1), channel_id=1, replica_groups=mesh['px'=16,'py'=16] {'px'}, dimensions={0} | all-to-all | bytes 1048576 | tf_op jit(solution)/shard_map/all_to_all | solution.py:374
  39.4 0.0 copy-done.2
  39.4 0.0 copy-done.3
  39.4 1.0 %mix.1 = bf16[8,2,16,256]{3,2,1,0:T(8,128)(2,1)S(1)} custom-call(bf16[16,64,256]{2,1,0:T(8,128)(2,1)S(1)} %all_to_all.16.got_ref, f32[16,512]{1,0:T(8,128)S(1)} %copy-done.2, f32[16,256]{1,0:T(8,128)S(1)} %copy-done.3, f32[16,32]{1,0:T(8,128)S(1)} %get-tuple-element.17.back_x_ref), custom_call_target="tpu_custom_call" | custom-call | tf_op jit(solution)/shard_map/mix/pallas_call | solution.py:375
  40.4 11.2 %all_to_all.17.own_ref = bf16[8,2,16,256]{3,2,1,0:T(8,128)(2,1)S(1)} all-to-all(bf16[8,2,16,256]{3,2,1,0:T(8,128)(2,1)S(1)} %mix.1), channel_id=1, replica_groups={{0,2,4,6,8,10,12,14},{1,3,5,7,9,11,13,15},{16,18,20,22,24,26,28,30},{17..., dimensions={0} | all-to-all | bytes 262144 | tf_op jit(solution)/shard_map/all_to_all | solution.py:383
  51.6 3.6 %collective-permute-start.1 = (bf16[8,2,16,256]{3,2,1,0:T(8,128)(2,1)S(1)}, bf16[8,2,16,256]{3,2,1,0:T(8,128)(2,1)S(1)}, u32[]{:S(2)}, u32[]{:S(2)}) collective-permute-start(bf16[8,2,16,256]{3,2,1,0:T(8,128)(2,1)S(1)} %all_to_all.17.own_ref), channel_id=1, source_target_pairs={{0,1},{1,0},{2,3},{3,2},{4,5},{5,4},{6,7},{7,6},{8,9},{9,8},{10,11... | collective-permute-start | bytes 393224 | tf_op jit(solution)/shard_map/ppermute | solution.py:384
  55.2 1.0 %collective-permute-done.1.other_ref = bf16[8,2,16,256]{3,2,1,0:T(8,128)(2,1)S(1)} collective-permute-done((bf16[8,2,16,256]{3,2,1,0:T(8,128)(2,1)S(1)}, bf16[8,2,16,256]{3,2,1,0:T(8,128)(2,1)S(1)}, u32[]{:S(2)}, u32[]{:S(2)}) %collective-permute-start.1) | collective-permute-done | bytes 131104 | tf_op jit(solution)/shard_map/ppermute | solution.py:384
  56.2 0.0 copy-done
  56.2 0.0 copy-done.1
  56.2 0.0 copy-done.4
  56.2 0.0 copy-done.5
  56.2 4.5 %inverse.1 = bf16[2,16,16,16,256]{4,3,2,1,0:T(8,128)(2,1)} custom-call(bf16[2,16,16,16,256]{4,3,2,1,0:T(8,128)(2,1)} %field_hbm.3, bf16[2,16,4,16,256]{4,3,2,1,0:T(8,128)(2,1)S(1)} %get-tuple-element.12.first_ref, bf16[2,16,4,16,256]{4,3,2,1,0:T(8,128)(2,1)S(1)} %get-tuple-element.13.second_ref, bf16[16,16]{1,0:T(8,128)(2,1)S(1)} %copy-done.4, ...), custom_call_target="tpu_custom_call" | custom-call | tf_op jit(solution)/shard_map/inverse/pallas_call | solution.py:385
  (2 shorter events, 0.1 us)
Async XLA Ops:
  0.1 39.3 %copy-start.2 = (f32[16,512]{1,0:T(8,128)S(1)}, f32[16,512]{1,0:T(8,128)}, u32[]{:S(2)}) copy-start(f32[16,512]{1,0:T(8,128)} %constant.30.clone.table_x_ref) | copy-start | bytes 98308
  0.1 39.3 %copy-start.3 = (f32[16,256]{1,0:T(8,128)S(1)}, f32[16,256]{1,0:T(8,128)}, u32[]{:S(2)}) copy-start(f32[16,256]{1,0:T(8,128)} %constant.31.clone.lanes_v_ref) | copy-start | bytes 49156
  0.1 56.1 %copy-start = (f32[32,256]{1,0:T(8,128)S(1)}, f32[32,256]{1,0:T(8,128)}, u32[]{:S(2)}) copy-start(f32[32,256]{1,0:T(8,128)} %constant.33.clone.table_z_ref) | copy-start | bytes 98308
  0.1 56.1 %copy-start.1 = (f32[16,512]{1,0:T(8,128)S(1)}, f32[16,512]{1,0:T(8,128)}, u32[]{:S(2)}) copy-start(f32[16,512]{1,0:T(8,128)} %constant.32.clone.expand_ref) | copy-start | bytes 98308
  0.1 56.1 %copy-start.4 = (bf16[16,16]{1,0:T(8,128)(2,1)S(1)}, bf16[16,16]{1,0:T(8,128)(2,1)}, u32[]{:S(2)}) copy-start(bf16[16,16]{1,0:T(8,128)(2,1)} %skip_ref.1) | copy-start | bytes 1540
  0.1 56.1 %copy-start.5 = (f32[16]{0:T(128)S(1)}, f32[16]{0:T(128)}, u32[]{:S(2)}) copy-start(f32[16]{0:T(128)} %param.16) | copy-start | bytes 196
  4.9 4.3 %collective-permute-start = (bf16[8,2,16,256]{3,2,1,0:T(8,128)(2,1)S(1)}, bf16[8,2,16,256]{3,2,1,0:T(8,128)(2,1)S(1)}, u32[]{:S(2)}, u32[]{:S(2)}) collective-permute-start(bf16[8,2,16,256]{3,2,1,0:T(8,128)(2,1)S(1)} %get-tuple-element.15), channel_id=1, source_target_pairs={{0,1},{1,0},{2,3},{3,2},{4,5},{5,4},{6,7},{7,6},{8,9},{9,8},{10,11... | collective-permute-start | bytes 393224 | tf_op jit(solution)/shard_map/ppermute | solution.py:363
  51.6 4.6 %collective-permute-start.1 = (bf16[8,2,16,256]{3,2,1,0:T(8,128)(2,1)S(1)}, bf16[8,2,16,256]{3,2,1,0:T(8,128)(2,1)S(1)}, u32[]{:S(2)}, u32[]{:S(2)}) collective-permute-start(bf16[8,2,16,256]{3,2,1,0:T(8,128)(2,1)S(1)} %all_to_all.17.own_ref), channel_id=1, source_target_pairs={{0,1},{1,0},{2,3},{3,2},{4,5},{5,4},{6,7},{7,6},{8,9},{9,8},{10,11... | collective-permute-start | bytes 393224 | tf_op jit(solution)/shard_map/ppermute | solution.py:384

commit v3 on v2

--- a/solution.py
+++ b/solution.py
@@ -21,6 +21,7 @@
 GROUP = 4
 GROUPS = BLOCK // GROUP
 AHEAD = 3
+ROWS = 128
 VMEM = 24 * 1024 * 1024
 CENTRE = (BLOCK - 1) / 2
 
@@ -254,8 +255,12 @@
     def fetch(g):
         return pltpu.make_async_copy(field_hbm.at[:, :, pl.ds(g * GROUP, GROUP)], held[g], arrived.at[g - 2])
 
-    def store(g):
-        return pltpu.make_async_copy(ready.at[g], out_ref.at[:, :, pl.ds(g * GROUP, GROUP)], sent.at[g])
+    def store(g, j, count):
+        return pltpu.make_async_copy(
+            ready.at[g, :, :, pl.ds(j, count)],
+            out_ref.at[:, :, pl.ds(g * GROUP + j, count)],
+            sent.at[g + j // 2],
+        )
 
     for g in (2, 3):
         fetch(g).start()
@@ -293,19 +298,29 @@
             rows = jnp.where(lane == 32 * j + 16, parts[j], rows)
         modes.append(rows.astype(jnp.bfloat16))
 
+    stores = []
     for g in range(GROUPS):
         if g >= 2:
             fetch(g).wait()
         for j in range(GROUP):
             for b in range(SLICES):
-                value = dot(modes[b][:, g * 128 : (g + 1) * 128], tables_z[j])
-                value = value + dot(skip, held[g][b, :, j].reshape(256, GRID))
-                half = 0.5 * value
-                value = half + half * lax.erf(value * math.sqrt(0.5))
-                ready[g, b, :, j] = value.astype(jnp.bfloat16).reshape(CHANNELS, BLOCK, GRID)
-        store(g).start()
-    for g in range(GROUPS):
-        store(g).wait()
+                lhs = modes[b][:, g * 128 : (g + 1) * 128]
+                for r in range(0, 256, ROWS):
+                    value = dot(lhs[r : r + ROWS], tables_z[j])
+                    value = value + dot(skip[r : r + ROWS], held[g][b, :, j].reshape(256, GRID))
+                    half = 0.5 * value
+                    value = half + half * lax.erf(value * math.sqrt(0.5))
+                    value = value.astype(jnp.bfloat16).reshape(ROWS // BLOCK, BLOCK, GRID)
+                    ready[g, b, r // BLOCK : (r + ROWS) // BLOCK, j] = value
+            if g == GROUPS - 1 and j % 2 == 1:
+                stores.append(store(g, j - 1, 2))
+            elif g < GROUPS - 1 and j == GROUP - 1:
+                stores.append(store(g, 0, GROUP))
+            else:
+                continue
+            stores[-1].start()
+    for copy in stores:
+        copy.wait()
 
 
 VM = pl.BlockSpec(memory_space=pltpu.VMEM)
@@ -392,7 +407,7 @@
             pltpu.VMEM((2, *planes), bf16),
             pltpu.VMEM((GROUPS, *planes), bf16),
             pltpu.SemaphoreType.DMA((2,)),
-            pltpu.SemaphoreType.DMA((GROUPS,)),
+            pltpu.SemaphoreType.DMA((GROUPS + 1,)),
         ],
         compiler_params=PARAMS,
     )(far[0], *held, skip_weight, bias.reshape(1, 16), own, other, back_y, t["expand_x"], t["inverse_z"])

time: 60.9 us -> 60.5 us (level)
  no operation moved by 1% of the time
where the time goes in v3:
time: 60.5 us; the launch traced here: 60.3 us
  blocking collectives  41.2 us (68%)
  Pallas kernels  10.1 us (17%)
  starting transfers between devices  6.92 us (11%)
  waiting for transfers between devices  1.97 us (3%)
    all_to_all x1, blocking collectives, on_device(): message = lax.all_to_all(message, 'px', 0, 0, tiled=True)  15.9 us
    all_to_all x1, blocking collectives, on_device(): sums = lax.all_to_all(sums, 'py', 0, 0, axis_index_groups=CHIPS, tiled=True)  14.1 us
    all_to_all x1, blocking collectives, on_device(): lax.all_to_all(message, 'py', 0, 0, axis_index_groups=CHIPS, tiled=True)  11.2 us
    pallas_call x1, Pallas kernels, on_device(): pl.pallas_call(forward_kernel, name='forward', in_specs=[SM] + [ANY] * 7,...  4.83 us
    pallas_call x1, Pallas kernels, on_device(): pl.pallas_call(inverse_kernel, name='inverse', in_specs=[ANY] + [VM] * 9,...  4.15 us
    ppermute x1, starting transfers between devices, on_device(): other = lax.ppermute(own, 'py', PAIR)  3.58 us
    ppermute x1, starting transfers between devices, on_device(): got = lax.ppermute(send, 'py', PAIR)  3.35 us
  transfers between devices with their start and end apart: 2, of which 2 were waited for; matrix products, arithmetic and copies ran while one was open for 0% of the time, Pallas kernels for 0%

profile of v3, /device:TPU:1, one launch (start us, length us, event | category | flops | bytes accessed | tf_op | source)
XLA Modules:
  0.0 60.3 jit_solution(1996622599898425164)
XLA Ops:
  0.0 0.1 pad_add_fusion.index_ref
  0.1 0.0 copy-start.2
  0.1 0.0 copy-start.3
  0.1 0.0 copy-start
  0.1 0.0 copy-start.1
  0.1 0.0 copy-start.4
  0.1 0.0 copy-start.5
  0.1 4.8 %forward.1 = (f32[8,2,16,256]{3,2,1,0:T(8,128)S(1)}, bf16[8,2,16,256]{3,2,1,0:T(8,128)(2,1)S(1)}, bf16[32,256]{1,0:T(8,128)(2,1)S(1)}, f32[16,512]{1,0:T(8,128)S...) custom-call(s32[2]{0:T(128)S(1)} %pad_add_fusion.index_ref, ...), custom_call_target="tpu_custom_call" | custom-call | tf_op jit(solution)/shard_map/forward/pallas_call | solution.py:352
  4.9 3.3 %collective-permute-start = (bf16[8,2,16,256]{3,2,1,0:T(8,128)(2,1)S(1)}, bf16[8,2,16,256]{3,2,1,0:T(8,128)(2,1)S(1)}, u32[]{:S(2)}, u32[]{:S(2)}) collective-permute-start(bf16[8,2,16,256]{3,2,1,0:T(8,128)(2,1)S(1)} %get-tuple-element.15), channel_id=1, source_target_pairs={{0,1},{1,0},{2,3},{3,2},{4,5},{5,4},{6,7},{7,6},{8,9},{9,8},{10,11... | collective-permute-start | bytes 393224 | tf_op jit(solution)/shard_map/ppermute | solution.py:378
  8.3 1.0 %collective-permute-done = bf16[8,2,16,256]{3,2,1,0:T(8,128)(2,1)S(1)} collective-permute-done((bf16[8,2,16,256]{3,2,1,0:T(8,128)(2,1)S(1)}, bf16[8,2,16,256]{3,2,1,0:T(8,128)(2,1)S(1)}, u32[]{:S(2)}, u32[]{:S(2)}) %collective-permute-start) | collective-permute-done | bytes 131104 | tf_op jit(solution)/shard_map/ppermute | solution.py:378
  9.3 14.1 %all_to_all.15.parts_ref = bf16[8,2,16,256]{3,2,1,0:T(8,128)(2,1)S(1)} all-to-all(bf16[8,2,16,256]{3,2,1,0:T(8,128)(2,1)S(1)} %add_convert_fusion), channel_id=1, replica_groups={{0,2,4,6,8,10,12,14},{1,3,5,7,9,11,13,15},{16,18,20,22,24,26,28,30},{17..., dimensions={0} | all-to-all | bytes 262144 | tf_op jit(solution)/shard_map/all_to_all | solution.py:380
  23.5 15.9 %all_to_all.16.got_ref = bf16[16,64,256]{2,1,0:T(8,128)(2,1)S(1)} all-to-all(bf16[16,64,256]{2,1,0:T(8,128)(2,1)S(1)} %sum.1), channel_id=1, replica_groups=mesh['px'=16,'py'=16] {'px'}, dimensions={0} | all-to-all | bytes 1048576 | tf_op jit(solution)/shard_map/all_to_all | solution.py:389
  39.4 0.0 copy-done.2
  39.4 0.0 copy-done.3
  39.4 1.0 %mix.1 = bf16[8,2,16,256]{3,2,1,0:T(8,128)(2,1)S(1)} custom-call(bf16[16,64,256]{2,1,0:T(8,128)(2,1)S(1)} %all_to_all.16.got_ref, f32[16,512]{1,0:T(8,128)S(1)} %copy-done.2, f32[16,256]{1,0:T(8,128)S(1)} %copy-done.3, f32[16,32]{1,0:T(8,128)S(1)} %get-tuple-element.17.back_x_ref), custom_call_target="tpu_custom_call" | custom-call | tf_op jit(solution)/shard_map/mix/pallas_call | solution.py:390
  40.4 11.2 %all_to_all.17.own_ref = bf16[8,2,16,256]{3,2,1,0:T(8,128)(2,1)S(1)} all-to-all(bf16[8,2,16,256]{3,2,1,0:T(8,128)(2,1)S(1)} %mix.1), channel_id=1, replica_groups={{0,2,4,6,8,10,12,14},{1,3,5,7,9,11,13,15},{16,18,20,22,24,26,28,30},{17..., dimensions={0} | all-to-all | bytes 262144 | tf_op jit(solution)/shard_map/all_to_all | solution.py:398
  51.6 3.6 %collective-permute-start.1 = (bf16[8,2,16,256]{3,2,1,0:T(8,128)(2,1)S(1)}, bf16[8,2,16,256]{3,2,1,0:T(8,128)(2,1)S(1)}, u32[]{:S(2)}, u32[]{:S(2)}) collective-permute-start(bf16[8,2,16,256]{3,2,1,0:T(8,128)(2,1)S(1)} %all_to_all.17.own_ref), channel_id=1, source_target_pairs={{0,1},{1,0},{2,3},{3,2},{4,5},{5,4},{6,7},{7,6},{8,9},{9,8},{10,11... | collective-permute-start | bytes 393224 | tf_op jit(solution)/shard_map/ppermute | solution.py:399
  55.2 1.0 %collective-permute-done.1.other_ref = bf16[8,2,16,256]{3,2,1,0:T(8,128)(2,1)S(1)} collective-permute-done((bf16[8,2,16,256]{3,2,1,0:T(8,128)(2,1)S(1)}, bf16[8,2,16,256]{3,2,1,0:T(8,128)(2,1)S(1)}, u32[]{:S(2)}, u32[]{:S(2)}) %collective-permute-start.1) | collective-permute-done | bytes 131104 | tf_op jit(solution)/shard_map/ppermute | solution.py:399
  56.2 0.0 copy-done
  56.2 0.0 copy-done.1
  56.2 0.0 copy-done.4
  56.2 0.0 copy-done.5
  56.2 4.2 %inverse.1 = bf16[2,16,16,16,256]{4,3,2,1,0:T(8,128)(2,1)} custom-call(bf16[2,16,16,16,256]{4,3,2,1,0:T(8,128)(2,1)} %field_hbm.3, bf16[2,16,4,16,256]{4,3,2,1,0:T(8,128)(2,1)S(1)} %get-tuple-element.12.first_ref, bf16[2,16,4,16,256]{4,3,2,1,0:T(8,128)(2,1)S(1)} %get-tuple-element.13.second_ref, bf16[16,16]{1,0:T(8,128)(2,1)S(1)} %copy-done.4, ...), custom_call_target="tpu_custom_call" | custom-call | tf_op jit(solution)/shard_map/inverse/pallas_call | solution.py:400
  (2 shorter events, 0.1 us)
Async XLA Ops:
  0.1 39.3 %copy-start.2 = (f32[16,512]{1,0:T(8,128)S(1)}, f32[16,512]{1,0:T(8,128)}, u32[]{:S(2)}) copy-start(f32[16,512]{1,0:T(8,128)} %constant.30.clone.table_x_ref) | copy-start | bytes 98308
  0.1 39.3 %copy-start.3 = (f32[16,256]{1,0:T(8,128)S(1)}, f32[16,256]{1,0:T(8,128)}, u32[]{:S(2)}) copy-start(f32[16,256]{1,0:T(8,128)} %constant.31.clone.lanes_v_ref) | copy-start | bytes 49156
  0.1 56.1 %copy-start = (f32[32,256]{1,0:T(8,128)S(1)}, f32[32,256]{1,0:T(8,128)}, u32[]{:S(2)}) copy-start(f32[32,256]{1,0:T(8,128)} %constant.33.clone.table_z_ref) | copy-start | bytes 98308
  0.1 56.1 %copy-start.1 = (f32[16,512]{1,0:T(8,128)S(1)}, f32[16,512]{1,0:T(8,128)}, u32[]{:S(2)}) copy-start(f32[16,512]{1,0:T(8,128)} %constant.32.clone.expand_ref) | copy-start | bytes 98308
  0.1 56.1 %copy-start.4 = (bf16[16,16]{1,0:T(8,128)(2,1)S(1)}, bf16[16,16]{1,0:T(8,128)(2,1)}, u32[]{:S(2)}) copy-start(bf16[16,16]{1,0:T(8,128)(2,1)} %skip_ref.1) | copy-start | bytes 1540
  0.1 56.1 %copy-start.5 = (f32[16]{0:T(128)S(1)}, f32[16]{0:T(128)}, u32[]{:S(2)}) copy-start(f32[16]{0:T(128)} %param.16) | copy-start | bytes 196
  4.9 4.3 %collective-permute-start = (bf16[8,2,16,256]{3,2,1,0:T(8,128)(2,1)S(1)}, bf16[8,2,16,256]{3,2,1,0:T(8,128)(2,1)S(1)}, u32[]{:S(2)}, u32[]{:S(2)}) collective-permute-start(bf16[8,2,16,256]{3,2,1,0:T(8,128)(2,1)S(1)} %get-tuple-element.15), channel_id=1, source_target_pairs={{0,1},{1,0},{2,3},{3,2},{4,5},{5,4},{6,7},{7,6},{8,9},{9,8},{10,11... | collective-permute-start | bytes 393224 | tf_op jit(solution)/shard_map/ppermute | solution.py:378
  51.6 4.6 %collective-permute-start.1 = (bf16[8,2,16,256]{3,2,1,0:T(8,128)(2,1)S(1)}, bf16[8,2,16,256]{3,2,1,0:T(8,128)(2,1)S(1)}, u32[]{:S(2)}, u32[]{:S(2)}) collective-permute-start(bf16[8,2,16,256]{3,2,1,0:T(8,128)(2,1)S(1)} %all_to_all.17.own_ref), channel_id=1, source_target_pairs={{0,1},{1,0},{2,3},{3,2},{4,5},{5,4},{6,7},{7,6},{8,9},{9,8},{10,11... | collective-permute-start | bytes 393224 | tf_op jit(solution)/shard_map/ppermute | solution.py:399

commit v4 on v3

--- a/solution.py
+++ b/solution.py
@@ -20,7 +20,6 @@
 Z_CHIPS = 8
 GROUP = 4
 GROUPS = BLOCK // GROUP
-AHEAD = 3
 ROWS = 128
 VMEM = 24 * 1024 * 1024
 CENTRE = (BLOCK - 1) / 2
@@ -111,24 +110,25 @@
     return jnp.where(keep, table, 0.0).astype(jnp.bfloat16)
 
 
-def turned(data):
-    return jnp.concatenate([data[:, HALF:], -data[:, :HALF]], axis=1)
-
-
 def with_turned(data):
-    return jnp.concatenate([data, turned(data)], axis=0).astype(jnp.bfloat16)
+    turned = jnp.concatenate([data[:, HALF:], -data[:, :HALF]], axis=1)
+    return jnp.concatenate([data, turned], axis=0).astype(jnp.bfloat16)
+
+
+def own_frequencies(table):
+    shape = (Z_CHIPS * 16, 512)
+    return masked(repeat_rows(table), iota(shape, 0) % 16 == iota(shape, 1) % 256 // 16)
 
 
 def forward_kernel(
-    index_ref, field_hbm, weight_hbm, table_z_hbm, lanes_x_hbm, table_y_hbm, back_y_hbm, back_x_hbm,
-    keep_ref, send_ref, packed_ref, back_y_ref, back_x_ref, first_ref, second_ref,
-    rest, weight_ref, table_z_ref, lanes_x_ref, table_y_ref, total, arrived, loaded,
+    index_ref, field_hbm, table_z_hbm, lanes_x_hbm, table_y_hbm, back_y_hbm, back_x_hbm,
+    sums_ref, send_ref, table_y_ref, back_y_ref, back_x_ref, first_ref, second_ref,
+    rest, table_z_ref, lanes_x_ref, total, arrived, loaded,
 ):
     small = [
         pltpu.make_async_copy(source, target, loaded.at[i])
         for i, (source, target) in enumerate(
             [
-                (weight_hbm, weight_ref),
                 (table_y_hbm.at[index_ref[1]], table_y_ref),
                 (table_z_hbm, table_z_ref),
                 (lanes_x_hbm, lanes_x_ref),
@@ -144,47 +144,42 @@
     def fetch(g):
         return pltpu.make_async_copy(field_hbm.at[:, :, pl.ds(g * GROUP, GROUP)], held[g], arrived.at[g])
 
-    for g in range(AHEAD):
+    for g in range(GROUPS):
         fetch(g).start()
+
+    small[0].wait()
+    table_y = own_frequencies(table_y_ref[Z_CHIPS:, :])
+    for copy in small[1:]:
+        copy.wait()
+
+    table = jnp.concatenate(
+        [(table_z_ref[...] * lanes_x_ref[x : x + 1, :]).astype(jnp.bfloat16) for x in range(BLOCK)], axis=0
+    )
+    for g in range(GROUPS):
+        fetch(g).wait()
+    data = jnp.concatenate(
+        [held[g][:, :, j].reshape(SLICES * 256, GRID) for g in range(GROUPS) for j in range(GROUP)], axis=1
+    )
+    total[...] = dot(data, table)
+
+    for b in range(SLICES):
+        sums = total[b * 256 : (b + 1) * 256, :]
+        sums_ref[b] = sums.astype(jnp.bfloat16)
+        send = dot(table_y, with_turned(sums))
+        send_ref[:, b] = send.reshape(Z_CHIPS, CHANNELS, LANES).astype(jnp.bfloat16)
+
+
+def keep_kernel(sums_ref, table_y_ref, weight_ref, keep_ref, packed_ref):
+    table_y = own_frequencies(table_y_ref[:Z_CHIPS, :])
+    for b in range(SLICES):
+        keep_ref[:, b] = dot(table_y, with_turned(sums_ref[b].astype(jnp.float32))).reshape(Z_CHIPS, CHANNELS, LANES)
 
     place = (iota((MODES, LANES), 0) == iota((MODES, LANES), 1) % MODES).astype(jnp.bfloat16)
     rows = iota((512, LANES), 0) % 16
     gather = (iota((32, 512), 0) == iota((32, 512), 1) // 16).astype(jnp.bfloat16)
-    small[0].wait()
     wide = dot(weight_ref[...].astype(jnp.bfloat16), place)
     wide = masked(wide, rows == iota((512, LANES), 1) // MODES)
     packed_ref[...] = dot(gather, wide).astype(jnp.bfloat16)
-
-    shape = (256, 512)
-    small[1].wait()
-    table_y = masked(
-        repeat_rows(table_y_ref[...]), iota(shape, 0) % 16 == iota(shape, 1) % 256 // 16
-    )
-    for copy in small[2:]:
-        copy.wait()
-
-    for g in range(GROUPS):
-        table = jnp.concatenate(
-            [
-                (table_z_ref[...] * lanes_x_ref[x : x + 1, :]).astype(jnp.bfloat16)
-                for x in range(g * GROUP, (g + 1) * GROUP)
-            ],
-            axis=0,
-        )
-        fetch(g).wait()
-        if g + AHEAD < GROUPS:
-            fetch(g + AHEAD).start()
-        data = jnp.concatenate(
-            [held[g][:, :, j].reshape(SLICES * 256, GRID) for j in range(GROUP)], axis=1
-        )
-        part = dot(data, table)
-        total[...] = part if g == 0 else total[...] + part
-
-    for b in range(SLICES):
-        sums = dot(table_y, with_turned(total[b * 256 : (b + 1) * 256, :]))
-        sums = sums.reshape(2, Z_CHIPS, CHANNELS, LANES)
-        keep_ref[:, b] = sums[0]
-        send_ref[:, b] = sums[1].astype(jnp.bfloat16)
 
 
 def sum_kernel(parts_ref, packed_ref, out_ref):
@@ -259,7 +254,7 @@
         return pltpu.make_async_copy(
             ready.at[g, :, :, pl.ds(j, count)],
             out_ref.at[:, :, pl.ds(g * GROUP + j, count)],
-            sent.at[g + j // 2],
+            sent.at[g + j],
         )
 
     for g in (2, 3):
@@ -312,9 +307,9 @@
                     value = half + half * lax.erf(value * math.sqrt(0.5))
                     value = value.astype(jnp.bfloat16).reshape(ROWS // BLOCK, BLOCK, GRID)
                     ready[g, b, r // BLOCK : (r + ROWS) // BLOCK, j] = value
-            if g == GROUPS - 1 and j % 2 == 1:
-                stores.append(store(g, j - 1, 2))
-            elif g < GROUPS - 1 and j == GROUP - 1:
+            if g == GROUPS - 1:
+                stores.append(store(g, j, 1))
+            elif j == GROUP - 1:
                 stores.append(store(g, 0, GROUP))
             else:
                 continue
@@ -345,19 +340,19 @@
     far = [
         pltpu.with_memory_space_constraint(a, pltpu.HBM)
         for a in (
-            field, spectral_weight.reshape(512, MODES), t["forward_z"], t["lanes_x"], t["forward_y"],
+            field, t["forward_z"], t["lanes_x"], t["forward_y"],
             t["inverse_y"], t["inverse_x"],
         )
     ]
-    keep, send, packed, back_y, back_x, *held = pl.pallas_call(
+    sums, send, table_y, back_y, back_x, *held = pl.pallas_call(
         forward_kernel,
         name="forward",
-        in_specs=[SM] + [ANY] * 7,
+        in_specs=[SM] + [ANY] * 6,
         out_specs=[VM] * 7,
         out_shape=[
-            shape_of(part, f32),
+            shape_of((SLICES, 256, LANES), bf16),
             shape_of(part, bf16),
-            shape_of((32, LANES), bf16),
+            shape_of((16, 512), f32),
             shape_of((16, 512), f32),
             shape_of((16, 32), f32),
             pltpu.VMEM(planes, bf16),
@@ -365,17 +360,24 @@
         ],
         scratch_shapes=[
             pltpu.VMEM((2, *planes), bf16),
-            pltpu.VMEM((512, MODES), f32),
             pltpu.VMEM((GRID, LANES), f32),
             pltpu.VMEM((BLOCK, LANES), f32),
-            pltpu.VMEM((16, 512), f32),
             pltpu.VMEM((512, LANES), f32),
             pltpu.SemaphoreType.DMA((GROUPS,)),
-            pltpu.SemaphoreType.DMA((6,)),
+            pltpu.SemaphoreType.DMA((5,)),
         ],
         compiler_params=PARAMS,
     )(place, *far)
     got = lax.ppermute(send, "py", PAIR)
+    keep, packed = pl.pallas_call(
+        keep_kernel,
+        name="keep",
+        in_specs=[VM, VM, VM],
+        out_specs=[VM, VM],
+        out_shape=[shape_of(part, f32), shape_of((32, LANES), bf16)],
+        compiler_params=PARAMS,
+        cost_estimate=pl.CostEstimate(flops=2 * 2 * 128 * 512 * 256, bytes_accessed=1 << 20, transcendentals=0),
+    )(sums, table_y, spectral_weight.reshape(512, MODES))
     sums = (keep + got.astype(f32)).astype(bf16)
     sums = lax.all_to_all(sums, "py", 0, 0, axis_index_groups=CHIPS, tiled=True)
     message = pl.pallas_call(
@@ -407,7 +409,7 @@
             pltpu.VMEM((2, *planes), bf16),
             pltpu.VMEM((GROUPS, *planes), bf16),
             pltpu.SemaphoreType.DMA((2,)),
-            pltpu.SemaphoreType.DMA((GROUPS + 1,)),
+            pltpu.SemaphoreType.DMA((GROUPS + GROUP - 1,)),
         ],
         compiler_params=PARAMS,
     )(far[0], *held, skip_weight, bias.reshape(1, 16), own, other, back_y, t["expand_x"], t["inverse_z"])

time: 60.5 us -> 60.3 us (level)
    pallas_call x1 -> x2, Pallas kernels: 4.83 us -> 5.02 us  [the longest x1 4.56 us: on_device(): pl.pallas_call(forward_kernel, name='forward', in_specs=[SM] + [ANY] * 6,...]
  transfers between devices with their start and end apart: 2 -> 2, of which waited for: 2 -> 2; matrix products, arithmetic and copies ran while one was open for 0% -> 0% of each run, Pallas kernels for 0% -> 1%
where the time goes in v4:
time: 60.3 us; the launch traced here: 60 us
  blocking collectives  41.2 us (68%)
  Pallas kernels  10.2 us (17%)
  starting transfers between devices  6.91 us (11%)
  waiting for transfers between devices  1.51 us (3%)
    all_to_all x1, blocking collectives, on_device(): message = lax.all_to_all(message, 'px', 0, 0, tiled=True)  15.9 us
    all_to_all x1, blocking collectives, on_device(): sums = lax.all_to_all(sums, 'py', 0, 0, axis_index_groups=CHIPS, tiled=True)  14.1 us
    all_to_all x1, blocking collectives, on_device(): lax.all_to_all(message, 'py', 0, 0, axis_index_groups=CHIPS, tiled=True)  11.2 us
    pallas_call x1, Pallas kernels, on_device(): pl.pallas_call(forward_kernel, name='forward', in_specs=[SM] + [ANY] * 6,...  4.56 us
    pallas_call x1, Pallas kernels, on_device(): pl.pallas_call(inverse_kernel, name='inverse', in_specs=[ANY] + [VM] * 9,...  4.07 us
    ppermute x1, starting transfers between devices, on_device(): other = lax.ppermute(own, 'py', PAIR)  3.58 us
    ppermute x1, starting transfers between devices, on_device(): got = lax.ppermute(send, 'py', PAIR)  3.33 us
  transfers between devices with their start and end apart: 2, of which 2 were waited for; matrix products, arithmetic and copies ran while one was open for 0% of the time, Pallas kernels for 1%

profile of v4, /device:TPU:1, one launch (start us, length us, event | category | flops | bytes accessed | tf_op | source)
XLA Modules:
  0.0 60.0 jit_solution(13240727467641311431)
XLA Ops:
  0.0 0.0 copy-start
  0.0 0.1 pad_add_fusion.index_ref
  0.1 0.0 copy-start.3
  0.1 0.0 copy-start.4
  0.1 0.0 copy-start.1
  0.1 0.0 copy-start.2
  0.1 0.0 copy-start.5
  0.1 0.0 copy-start.6
  0.1 4.6 %forward.1 = (bf16[2,256,256]{2,1,0:T(8,128)(2,1)S(1)}, bf16[8,2,16,256]{3,2,1,0:T(8,128)(2,1)S(1)}, f32[16,512]{1,0:T(8,128)S(1)}, f32[16,512]{1,0:T(8,128)S(1)...) custom-call(s32[2]{0:T(128)S(1)} %pad_add_fusion.index_ref, ...), custom_call_target="tpu_custom_call" | custom-call | tf_op jit(solution)/shard_map/forward/pallas_call | solution.py:347
  4.7 3.3 %collective-permute-start = (bf16[8,2,16,256]{3,2,1,0:T(8,128)(2,1)S(1)}, bf16[8,2,16,256]{3,2,1,0:T(8,128)(2,1)S(1)}, u32[]{:S(2)}, u32[]{:S(2)}) collective-permute-start(bf16[8,2,16,256]{3,2,1,0:T(8,128)(2,1)S(1)} %get-tuple-element.19), channel_id=1, source_target_pairs={{0,1},{1,0},{2,3},{3,2},{4,5},{5,4},{6,7},{7,6},{8,9},{9,8},{10,11... | collective-permute-start | bytes 393224 | tf_op jit(solution)/shard_map/ppermute | solution.py:371
  8.0 0.0 copy-done
  8.0 0.5 keep.1
  8.5 0.5 collective-permute-done
  9.0 14.1 %all_to_all.15.parts_ref = bf16[8,2,16,256]{3,2,1,0:T(8,128)(2,1)S(1)} all-to-all(bf16[8,2,16,256]{3,2,1,0:T(8,128)(2,1)S(1)} %add_convert_fusion), channel_id=1, replica_groups={{0,2,4,6,8,10,12,14},{1,3,5,7,9,11,13,15},{16,18,20,22,24,26,28,30},{17..., dimensions={0} | all-to-all | bytes 262144 | tf_op jit(solution)/shard_map/all_to_all | solution.py:382
  23.2 15.9 %all_to_all.16.got_ref = bf16[16,64,256]{2,1,0:T(8,128)(2,1)S(1)} all-to-all(bf16[16,64,256]{2,1,0:T(8,128)(2,1)S(1)} %sum.1), channel_id=1, replica_groups=mesh['px'=16,'py'=16] {'px'}, dimensions={0} | all-to-all | bytes 1048576 | tf_op jit(solution)/shard_map/all_to_all | solution.py:391
  39.1 0.0 copy-done.3
  39.1 0.0 copy-done.4
  39.1 1.0 %mix.1 = bf16[8,2,16,256]{3,2,1,0:T(8,128)(2,1)S(1)} custom-call(bf16[16,64,256]{2,1,0:T(8,128)(2,1)S(1)} %all_to_all.16.got_ref, f32[16,512]{1,0:T(8,128)S(1)} %copy-done.3, f32[16,256]{1,0:T(8,128)S(1)} %copy-done.4, f32[16,32]{1,0:T(8,128)S(1)} %get-tuple-element.21.back_x_ref), custom_call_target="tpu_custom_call" | custom-call | tf_op jit(solution)/shard_map/mix/pallas_call | solution.py:392
  40.2 11.2 %all_to_all.17.own_ref = bf16[8,2,16,256]{3,2,1,0:T(8,128)(2,1)S(1)} all-to-all(bf16[8,2,16,256]{3,2,1,0:T(8,128)(2,1)S(1)} %mix.1), channel_id=1, replica_groups={{0,2,4,6,8,10,12,14},{1,3,5,7,9,11,13,15},{16,18,20,22,24,26,28,30},{17..., dimensions={0} | all-to-all | bytes 262144 | tf_op jit(solution)/shard_map/all_to_all | solution.py:400
  51.4 3.6 %collective-permute-start.1 = (bf16[8,2,16,256]{3,2,1,0:T(8,128)(2,1)S(1)}, bf16[8,2,16,256]{3,2,1,0:T(8,128)(2,1)S(1)}, u32[]{:S(2)}, u32[]{:S(2)}) collective-permute-start(bf16[8,2,16,256]{3,2,1,0:T(8,128)(2,1)S(1)} %all_to_all.17.own_ref), channel_id=1, source_target_pairs={{0,1},{1,0},{2,3},{3,2},{4,5},{5,4},{6,7},{7,6},{8,9},{9,8},{10,11... | collective-permute-start | bytes 393224 | tf_op jit(solution)/shard_map/ppermute | solution.py:401
  54.9 1.0 %collective-permute-done.1.other_ref = bf16[8,2,16,256]{3,2,1,0:T(8,128)(2,1)S(1)} collective-permute-done((bf16[8,2,16,256]{3,2,1,0:T(8,128)(2,1)S(1)}, bf16[8,2,16,256]{3,2,1,0:T(8,128)(2,1)S(1)}, u32[]{:S(2)}, u32[]{:S(2)}) %collective-permute-start.1) | collective-permute-done | bytes 131104 | tf_op jit(solution)/shard_map/ppermute | solution.py:401
  55.9 0.0 copy-done.1
  55.9 0.0 copy-done.2
  55.9 0.0 copy-done.5
  55.9 0.0 copy-done.6
  55.9 4.1 %inverse.1 = bf16[2,16,16,16,256]{4,3,2,1,0:T(8,128)(2,1)} custom-call(bf16[2,16,16,16,256]{4,3,2,1,0:T(8,128)(2,1)} %field_hbm.3, bf16[2,16,4,16,256]{4,3,2,1,0:T(8,128)(2,1)S(1)} %get-tuple-element.14.first_ref, bf16[2,16,4,16,256]{4,3,2,1,0:T(8,128)(2,1)S(1)} %get-tuple-element.15.second_ref, bf16[16,16]{1,0:T(8,128)(2,1)S(1)} %copy-done.5, ...), custom_call_target="tpu_custom_call" | custom-call | tf_op jit(solution)/shard_map/inverse/pallas_call | solution.py:402
  (2 shorter events, 0.1 us)
Async XLA Ops:
  0.0 8.0 %copy-start = (f32[1,1,2,16,16,16]{5,4,3,2,1,0:T(8,128)S(1)}, f32[1,1,2,16,16,16]{5,4,3,2,1,0:T(8,128)}, u32[]{:S(2)}) copy-start(f32[1,1,2,16,16,16]{5,4,3,2,1,0:T(8,128)} %param.14) | copy-start | bytes 98308
  0.1 39.1 %copy-start.3 = (f32[16,512]{1,0:T(8,128)S(1)}, f32[16,512]{1,0:T(8,128)}, u32[]{:S(2)}) copy-start(f32[16,512]{1,0:T(8,128)} %constant.30.clone.table_x_ref) | copy-start | bytes 98308
  0.1 39.1 %copy-start.4 = (f32[16,256]{1,0:T(8,128)S(1)}, f32[16,256]{1,0:T(8,128)}, u32[]{:S(2)}) copy-start(f32[16,256]{1,0:T(8,128)} %constant.31.clone.lanes_v_ref) | copy-start | bytes 49156
  0.1 55.9 %copy-start.1 = (f32[32,256]{1,0:T(8,128)S(1)}, f32[32,256]{1,0:T(8,128)}, u32[]{:S(2)}) copy-start(f32[32,256]{1,0:T(8,128)} %constant.33.clone.table_z_ref) | copy-start | bytes 98308
  0.1 55.9 %copy-start.2 = (f32[16,512]{1,0:T(8,128)S(1)}, f32[16,512]{1,0:T(8,128)}, u32[]{:S(2)}) copy-start(f32[16,512]{1,0:T(8,128)} %constant.32.clone.expand_ref) | copy-start | bytes 98308
  0.1 55.9 %copy-start.5 = (bf16[16,16]{1,0:T(8,128)(2,1)S(1)}, bf16[16,16]{1,0:T(8,128)(2,1)}, u32[]{:S(2)}) copy-start(bf16[16,16]{1,0:T(8,128)(2,1)} %skip_ref.1) | copy-start | bytes 1540
  0.1 55.8 %copy-start.6 = (f32[16]{0:T(128)S(1)}, f32[16]{0:T(128)}, u32[]{:S(2)}) copy-start(f32[16]{0:T(128)} %param.16) | copy-start | bytes 196
  4.7 4.3 %collective-permute-start = (bf16[8,2,16,256]{3,2,1,0:T(8,128)(2,1)S(1)}, bf16[8,2,16,256]{3,2,1,0:T(8,128)(2,1)S(1)}, u32[]{:S(2)}, u32[]{:S(2)}) collective-permute-start(bf16[8,2,16,256]{3,2,1,0:T(8,128)(2,1)S(1)} %get-tuple-element.19), channel_id=1, source_target_pairs={{0,1},{1,0},{2,3},{3,2},{4,5},{5,4},{6,7},{7,6},{8,9},{9,8},{10,11... | collective-permute-start | bytes 393224 | tf_op jit(solution)/shard_map/ppermute | solution.py:371
  51.4 4.6 %collective-permute-start.1 = (bf16[8,2,16,256]{3,2,1,0:T(8,128)(2,1)S(1)}, bf16[8,2,16,256]{3,2,1,0:T(8,128)(2,1)S(1)}, u32[]{:S(2)}, u32[]{:S(2)}) collective-permute-start(bf16[8,2,16,256]{3,2,1,0:T(8,128)(2,1)S(1)} %all_to_all.17.own_ref), channel_id=1, source_target_pairs={{0,1},{1,0},{2,3},{3,2},{4,5},{5,4},{6,7},{7,6},{8,9},{9,8},{10,11... | collective-permute-start | bytes 393224 | tf_op jit(solution)/shard_map/ppermute | solution.py:401

commit v5 on v4

--- a/solution.py
+++ b/solution.py
@@ -122,8 +122,8 @@
 
 def forward_kernel(
     index_ref, field_hbm, table_z_hbm, lanes_x_hbm, table_y_hbm, back_y_hbm, back_x_hbm,
-    sums_ref, send_ref, table_y_ref, back_y_ref, back_x_ref, first_ref, second_ref,
-    rest, table_z_ref, lanes_x_ref, total, arrived, loaded,
+    sums_ref, send_ref, table_y_ref, back_y_ref, back_x_ref, held0, held1, held2, held3,
+    table_z_ref, lanes_x_ref, total, arrived, loaded,
 ):
     small = [
         pltpu.make_async_copy(source, target, loaded.at[i])
@@ -139,7 +139,7 @@
     ]
     for copy in small:
         copy.start()
-    held = [first_ref, second_ref, rest.at[0], rest.at[1]]
+    held = [held0, held1, held2, held3]
 
     def fetch(g):
         return pltpu.make_async_copy(field_hbm.at[:, :, pl.ds(g * GROUP, GROUP)], held[g], arrived.at[g])
@@ -240,15 +240,43 @@
         out_ref[:, b] = jnp.broadcast_to(message[None], (Z_CHIPS, CHANNELS, LANES))
 
 
+def prepare_kernel(
+    skip_ref, bias_ref, own_ref, table_y_ref, basis_ref, table_z_ref,
+    left_ref, parts_ref, rows_z_ref, expand_ref, other_y_ref, modes_ref,
+):
+    shape = (256, 256)
+    place = (iota((16, 256), 0) == iota((16, 256), 1) // 16).astype(jnp.bfloat16)
+    skip = repeat_rows(dot(skip_ref[...], place))
+    left_ref[...] = masked(skip, iota(shape, 0) % 16 == iota(shape, 1) % 16)
+    one = iota((256, 16), 0) // 16 == iota((256, 16), 1)
+    bias = jnp.sum(jnp.where(one, bias_ref[...], 0.0), axis=1, keepdims=True)
+    for j in range(3):
+        part = bias.astype(jnp.bfloat16).astype(jnp.float32)
+        parts_ref[j] = jnp.broadcast_to(part, (256, 128))
+        bias = bias - part
+
+    shape = (2 * MODES, GRID)
+    ones = jnp.where(iota(shape, 0) == MODES, 1.0, 0.0)
+    for j in range(GROUP):
+        blocks = [ones, ones, ones, jnp.zeros(shape, jnp.float32)]
+        blocks[j] = blocks[j] + table_z_ref[...]
+        rows_z_ref[j] = jnp.concatenate(blocks, axis=0).astype(jnp.bfloat16)
+
+    shape = (256, 512)
+    table = masked(tile_rows(table_y_ref[...]), iota(shape, 0) // 16 == iota(shape, 1) % 16)
+    expand_ref[...] = masked(repeat_rows(basis_ref[...]), iota(shape, 0) % 16 == iota(shape, 1) % 16)
+    own = jnp.concatenate([table[:, 0:128], table[:, 256:384]], axis=1)
+    other_y_ref[...] = jnp.concatenate([table[:, 128:256], table[:, 384:512]], axis=1)
+    for b in range(SLICES):
+        data = own_ref[:, b].reshape(128, LANES).astype(jnp.float32)
+        modes_ref[b] = dot(own, with_turned(data))
+
+
 def inverse_kernel(
-    field_hbm, first_ref, second_ref, skip_ref, bias_ref, own_ref, other_ref,
-    table_y_ref, expand_ref, table_z_ref,
-    out_ref, rest, ready, arrived, sent,
+    held0, held1, held2, held3, left_ref, parts_ref, table_z_ref, expand_ref, table_y_ref, modes_ref, other_ref,
+    out_ref, ready, sent,
 ):
-    held = [first_ref, second_ref, rest.at[0], rest.at[1]]
-
-    def fetch(g):
-        return pltpu.make_async_copy(field_hbm.at[:, :, pl.ds(g * GROUP, GROUP)], held[g], arrived.at[g - 2])
+    held = [held0, held1, held2, held3]
 
     def store(g, j, count):
         return pltpu.make_async_copy(
@@ -257,46 +285,21 @@
             sent.at[g + j],
         )
 
-    for g in (2, 3):
-        fetch(g).start()
-
-    shape = (256, 256)
-    place = (iota((16, 256), 0) == iota((16, 256), 1) // 16).astype(jnp.bfloat16)
-    skip = repeat_rows(dot(skip_ref[...], place))
-    skip = masked(skip, iota(shape, 0) % 16 == iota(shape, 1) % 16)
-    one = iota((256, 16), 0) // 16 == iota((256, 16), 1)
-    bias = jnp.sum(jnp.where(one, bias_ref[...], 0.0), axis=1, keepdims=True)
-    parts = []
-    for _ in range(3):
-        parts.append(bias.astype(jnp.bfloat16).astype(jnp.float32))
-        bias = bias - parts[-1]
-
-    shape = (2 * MODES, GRID)
-    ones = jnp.where(iota(shape, 0) == MODES, 1.0, 0.0)
-    tables_z = []
-    for j in range(GROUP):
-        blocks = [ones, ones, ones, jnp.zeros(shape, jnp.float32)]
-        blocks[j] = blocks[j] + table_z_ref[...]
-        tables_z.append(jnp.concatenate(blocks, axis=0).astype(jnp.bfloat16))
-
-    shape = (256, 512)
-    table_y = masked(tile_rows(table_y_ref[...]), iota(shape, 0) // 16 == iota(shape, 1) % 16)
-    expand = masked(repeat_rows(expand_ref[...]), iota(shape, 0) % 16 == iota(shape, 1) % 16)
-    lane = iota(shape, 1) % 128
+    skip = left_ref[...]
+    tables_z = [table_z_ref[j] for j in range(GROUP)]
+    lane = iota((256, 512), 1) % 128
     modes = []
     for b in range(SLICES):
-        data = [ref[:, b].reshape(128, LANES) for ref in (own_ref, other_ref)]
-        data = jnp.concatenate(data, axis=0).astype(jnp.float32)
-        rows = dot(table_y, with_turned(data)).astype(jnp.bfloat16)
-        rows = dot(rows, expand)
+        data = other_ref[:, b].reshape(128, LANES).astype(jnp.float32)
+        rows = modes_ref[b] + dot(table_y_ref[...], with_turned(data))
+        rows = dot(rows.astype(jnp.bfloat16), expand_ref[...])
         for j in range(3):
-            rows = jnp.where(lane == 32 * j + 16, parts[j], rows)
+            part = jnp.concatenate([parts_ref[j]] * 4, axis=1)
+            rows = jnp.where(lane == 32 * j + 16, part, rows)
         modes.append(rows.astype(jnp.bfloat16))
 
     stores = []
     for g in range(GROUPS):
-        if g >= 2:
-            fetch(g).wait()
         for j in range(GROUP):
             for b in range(SLICES):
                 lhs = modes[b][:, g * 128 : (g + 1) * 128]
@@ -348,18 +351,16 @@
         forward_kernel,
         name="forward",
         in_specs=[SM] + [ANY] * 6,
-        out_specs=[VM] * 7,
+        out_specs=[VM] * (5 + GROUPS),
         out_shape=[
             shape_of((SLICES, 256, LANES), bf16),
             shape_of(part, bf16),
             shape_of((16, 512), f32),
             shape_of((16, 512), f32),
             shape_of((16, 32), f32),
-            pltpu.VMEM(planes, bf16),
-            pltpu.VMEM(planes, bf16),
+            *[pltpu.VMEM(planes, bf16)] * GROUPS,
         ],
         scratch_shapes=[
-            pltpu.VMEM((2, *planes), bf16),
             pltpu.VMEM((GRID, LANES), f32),
             pltpu.VMEM((BLOCK, LANES), f32),
             pltpu.VMEM((512, LANES), f32),
@@ -399,20 +400,34 @@
     )(message, t["forward_x"], t["lanes_v"], back_x)
     own = lax.all_to_all(message, "py", 0, 0, axis_index_groups=CHIPS, tiled=True)
     other = lax.ppermute(own, "py", PAIR)
+    prepared = pl.pallas_call(
+        prepare_kernel,
+        name="prepare",
+        in_specs=[VM] * 6,
+        out_specs=[VM] * 6,
+        out_shape=[
+            shape_of((256, 256), bf16),
+            shape_of((3, 256, 128), f32),
+            shape_of((GROUP, 128, GRID), bf16),
+            shape_of((LANES, 512), bf16),
+            shape_of((256, 256), bf16),
+            shape_of((SLICES, 256, LANES), f32),
+        ],
+        compiler_params=PARAMS,
+        cost_estimate=pl.CostEstimate(flops=2 * 2 * 256 * 256 * 256, bytes_accessed=1 << 20, transcendentals=0),
+    )(skip_weight, bias.reshape(1, 16), own, back_y, t["expand_x"], t["inverse_z"])
     return pl.pallas_call(
         inverse_kernel,
         name="inverse",
-        in_specs=[ANY] + [VM] * 9,
+        in_specs=[VM] * (7 + GROUPS),
         out_specs=ANY,
         out_shape=shape_of(field.shape, bf16),
         scratch_shapes=[
-            pltpu.VMEM((2, *planes), bf16),
             pltpu.VMEM((GROUPS, *planes), bf16),
-            pltpu.SemaphoreType.DMA((2,)),
             pltpu.SemaphoreType.DMA((GROUPS + GROUP - 1,)),
         ],
         compiler_params=PARAMS,
-    )(far[0], *held, skip_weight, bias.reshape(1, 16), own, other, back_y, t["expand_x"], t["inverse_z"])
+    )(*held, *prepared, other)
 
 
 def solution(mesh):

time: 60.3 us -> 59.8 us (level)
    pallas_call x1 -> x2, Pallas kernels: 4.07 us -> 3.94 us  [the longest x1 3.62 us: on_device(): pl.pallas_call(inverse_kernel, name='inverse', in_specs=[VM] * (7 + GROUP...]
where the time goes in v5:
time: 59.8 us; the launch traced here: 59.5 us
  blocking collectives  41.2 us (69%)
  Pallas kernels  10 us (17%)
  starting transfers between devices  6.91 us (12%)
  waiting for transfers between devices  1.17 us (2%)
    all_to_all x1, blocking collectives, on_device(): message = lax.all_to_all(message, 'px', 0, 0, tiled=True)  15.9 us
    all_to_all x1, blocking collectives, on_device(): sums = lax.all_to_all(sums, 'py', 0, 0, axis_index_groups=CHIPS, tiled=True)  14.1 us
    all_to_all x1, blocking collectives, on_device(): lax.all_to_all(message, 'py', 0, 0, axis_index_groups=CHIPS, tiled=True)  11.2 us
    pallas_call x1, Pallas kernels, on_device(): pl.pallas_call(forward_kernel, name='forward', in_specs=[SM] + [ANY] * 6,...  4.53 us
    pallas_call x1, Pallas kernels, on_device(): pl.pallas_call(inverse_kernel, name='inverse', in_specs=[VM] * (7 + GROUP...  3.62 us
    ppermute x1, starting transfers between devices, on_device(): other = lax.ppermute(own, 'py', PAIR)  3.58 us
    ppermute x1, starting transfers between devices, on_device(): got = lax.ppermute(send, 'py', PAIR)  3.33 us
  transfers between devices with their start and end apart: 2, of which 2 were waited for; matrix products, arithmetic and copies ran while one was open for 0% of the time, Pallas kernels for 1%

profile of v5, /device:TPU:1, one launch (start us, length us, event | category | flops | bytes accessed | tf_op | source)
XLA Modules:
  0.0 59.5 jit_solution(10524014777872620042)
XLA Ops:
  0.0 0.0 copy-start
  0.0 0.1 pad_add_fusion.index_ref
  0.1 0.0 copy-start.1
  0.1 0.0 copy-start.2
  0.1 0.0 copy-start.3
  0.1 0.0 copy-start.4
  0.1 0.0 copy-start.5
  0.1 0.0 copy-start.6
  0.1 4.5 %forward.1 = (bf16[2,256,256]{2,1,0:T(8,128)(2,1)S(1)}, bf16[8,2,16,256]{3,2,1,0:T(8,128)(2,1)S(1)}, f32[16,512]{1,0:T(8,128)S(1)}, f32[16,512]{1,0:T(8,128)S(1)...) custom-call(s32[2]{0:T(128)S(1)} %pad_add_fusion.index_ref, ...), custom_call_target="tpu_custom_call" | custom-call | tf_op jit(solution)/shard_map/forward/pallas_call | solution.py:350
  4.7 3.3 %collective-permute-start = (bf16[8,2,16,256]{3,2,1,0:T(8,128)(2,1)S(1)}, bf16[8,2,16,256]{3,2,1,0:T(8,128)(2,1)S(1)}, u32[]{:S(2)}, u32[]{:S(2)}) collective-permute-start(bf16[8,2,16,256]{3,2,1,0:T(8,128)(2,1)S(1)} %get-tuple-element.29), channel_id=1, source_target_pairs={{0,1},{1,0},{2,3},{3,2},{4,5},{5,4},{6,7},{7,6},{8,9},{9,8},{10,11... | collective-permute-start | bytes 393224 | tf_op jit(solution)/shard_map/ppermute | solution.py:372
  8.0 0.0 copy-done
  8.0 0.5 keep.1
  8.5 0.5 collective-permute-done
  9.0 14.1 %all_to_all.15.parts_ref = bf16[8,2,16,256]{3,2,1,0:T(8,128)(2,1)S(1)} all-to-all(bf16[8,2,16,256]{3,2,1,0:T(8,128)(2,1)S(1)} %add_convert_fusion), channel_id=1, replica_groups={{0,2,4,6,8,10,12,14},{1,3,5,7,9,11,13,15},{16,18,20,22,24,26,28,30},{17..., dimensions={0} | all-to-all | bytes 262144 | tf_op jit(solution)/shard_map/all_to_all | solution.py:383
  23.2 15.9 %all_to_all.16.got_ref = bf16[16,64,256]{2,1,0:T(8,128)(2,1)S(1)} all-to-all(bf16[16,64,256]{2,1,0:T(8,128)(2,1)S(1)} %sum.1), channel_id=1, replica_groups=mesh['px'=16,'py'=16] {'px'}, dimensions={0} | all-to-all | bytes 1048576 | tf_op jit(solution)/shard_map/all_to_all | solution.py:392
  39.1 0.0 copy-done.1
  39.1 0.0 copy-done.2
  39.1 1.0 %mix.1 = bf16[8,2,16,256]{3,2,1,0:T(8,128)(2,1)S(1)} custom-call(bf16[16,64,256]{2,1,0:T(8,128)(2,1)S(1)} %all_to_all.16.got_ref, f32[16,512]{1,0:T(8,128)S(1)} %copy-done.1, f32[16,256]{1,0:T(8,128)S(1)} %copy-done.2, f32[16,32]{1,0:T(8,128)S(1)} %get-tuple-element.31.back_x_ref), custom_call_target="tpu_custom_call" | custom-call | tf_op jit(solution)/shard_map/mix/pallas_call | solution.py:393
  40.2 11.2 %all_to_all.17.own_ref = bf16[8,2,16,256]{3,2,1,0:T(8,128)(2,1)S(1)} all-to-all(bf16[8,2,16,256]{3,2,1,0:T(8,128)(2,1)S(1)} %mix.1), channel_id=1, replica_groups={{0,2,4,6,8,10,12,14},{1,3,5,7,9,11,13,15},{16,18,20,22,24,26,28,30},{17..., dimensions={0} | all-to-all | bytes 262144 | tf_op jit(solution)/shard_map/all_to_all | solution.py:401
  51.4 3.6 %collective-permute-start.1 = (bf16[8,2,16,256]{3,2,1,0:T(8,128)(2,1)S(1)}, bf16[8,2,16,256]{3,2,1,0:T(8,128)(2,1)S(1)}, u32[]{:S(2)}, u32[]{:S(2)}) collective-permute-start(bf16[8,2,16,256]{3,2,1,0:T(8,128)(2,1)S(1)} %all_to_all.17.own_ref), channel_id=1, source_target_pairs={{0,1},{1,0},{2,3},{3,2},{4,5},{5,4},{6,7},{7,6},{8,9},{9,8},{10,11... | collective-permute-start | bytes 393224 | tf_op jit(solution)/shard_map/ppermute | solution.py:402
  54.9 0.0 copy-done.3
  54.9 0.0 copy-done.4
  54.9 0.0 copy-done.5
  54.9 0.0 copy-done.6
  54.9 0.3 prepare.1
  55.3 0.7 %collective-permute-done.1.other_ref = bf16[8,2,16,256]{3,2,1,0:T(8,128)(2,1)S(1)} collective-permute-done((bf16[8,2,16,256]{3,2,1,0:T(8,128)(2,1)S(1)}, bf16[8,2,16,256]{3,2,1,0:T(8,128)(2,1)S(1)}, u32[]{:S(2)}, u32[]{:S(2)}) %collective-permute-start.1) | collective-permute-done | bytes 131104 | tf_op jit(solution)/shard_map/ppermute | solution.py:402
  55.9 3.6 %inverse.1 = bf16[2,16,16,16,256]{4,3,2,1,0:T(8,128)(2,1)} custom-call(bf16[2,16,4,16,256]{4,3,2,1,0:T(8,128)(2,1)S(1)} %get-tuple-element.22.held0, bf16[2,16,4,16,256]{4,3,2,1,0:T(8,128)(2,1)S(1)} %get-tuple-element.23.held1, bf16[2,16,4,16,256]{4,3,2,1,0:T(8,128)(2,1)S(1)} %get-tuple-element.24.held2, ...), custom_call_target="tpu_custom_call" | custom-call | tf_op jit(solution)/shard_map/inverse/pallas_call | solution.py:419
  (2 shorter events, 0.1 us)
Async XLA Ops:
  0.0 8.0 %copy-start = (f32[1,1,2,16,16,16]{5,4,3,2,1,0:T(8,128)S(1)}, f32[1,1,2,16,16,16]{5,4,3,2,1,0:T(8,128)}, u32[]{:S(2)}) copy-start(f32[1,1,2,16,16,16]{5,4,3,2,1,0:T(8,128)} %param.14) | copy-start | bytes 98308
  0.1 39.0 %copy-start.1 = (f32[16,512]{1,0:T(8,128)S(1)}, f32[16,512]{1,0:T(8,128)}, u32[]{:S(2)}) copy-start(f32[16,512]{1,0:T(8,128)} %constant.30.clone.table_x_ref) | copy-start | bytes 98308
  0.1 39.0 %copy-start.2 = (f32[16,256]{1,0:T(8,128)S(1)}, f32[16,256]{1,0:T(8,128)}, u32[]{:S(2)}) copy-start(f32[16,256]{1,0:T(8,128)} %constant.31.clone.lanes_v_ref) | copy-start | bytes 49156
  0.1 54.8 %copy-start.3 = (bf16[16,16]{1,0:T(8,128)(2,1)S(1)}, bf16[16,16]{1,0:T(8,128)(2,1)}, u32[]{:S(2)}) copy-start(bf16[16,16]{1,0:T(8,128)(2,1)} %skip_ref.1) | copy-start | bytes 1540
  0.1 54.9 %copy-start.4 = (f32[16]{0:T(128)S(1)}, f32[16]{0:T(128)}, u32[]{:S(2)}) copy-start(f32[16]{0:T(128)} %param.16) | copy-start | bytes 196
  0.1 54.8 %copy-start.5 = (f32[32,256]{1,0:T(8,128)S(1)}, f32[32,256]{1,0:T(8,128)}, u32[]{:S(2)}) copy-start(f32[32,256]{1,0:T(8,128)} %constant.33.clone.table_z_ref) | copy-start | bytes 98308
  0.1 54.8 %copy-start.6 = (f32[16,512]{1,0:T(8,128)S(1)}, f32[16,512]{1,0:T(8,128)}, u32[]{:S(2)}) copy-start(f32[16,512]{1,0:T(8,128)} %constant.32.clone.basis_ref) | copy-start | bytes 98308
  4.7 4.3 %collective-permute-start = (bf16[8,2,16,256]{3,2,1,0:T(8,128)(2,1)S(1)}, bf16[8,2,16,256]{3,2,1,0:T(8,128)(2,1)S(1)}, u32[]{:S(2)}, u32[]{:S(2)}) collective-permute-start(bf16[8,2,16,256]{3,2,1,0:T(8,128)(2,1)S(1)} %get-tuple-element.29), channel_id=1, source_target_pairs={{0,1},{1,0},{2,3},{3,2},{4,5},{5,4},{6,7},{7,6},{8,9},{9,8},{10,11... | collective-permute-start | bytes 393224 | tf_op jit(solution)/shard_map/ppermute | solution.py:372
  51.4 4.6 %collective-permute-start.1 = (bf16[8,2,16,256]{3,2,1,0:T(8,128)(2,1)S(1)}, bf16[8,2,16,256]{3,2,1,0:T(8,128)(2,1)S(1)}, u32[]{:S(2)}, u32[]{:S(2)}) collective-permute-start(bf16[8,2,16,256]{3,2,1,0:T(8,128)(2,1)S(1)} %all_to_all.17.own_ref), channel_id=1, source_target_pairs={{0,1},{1,0},{2,3},{3,2},{4,5},{5,4},{6,7},{7,6},{8,9},{9,8},{10,11... | collective-permute-start | bytes 393224 | tf_op jit(solution)/shard_map/ppermute | solution.py:402

commit v6 on v5

--- a/solution.py
+++ b/solution.py
@@ -23,6 +23,8 @@
 ROWS = 128
 VMEM = 24 * 1024 * 1024
 CENTRE = (BLOCK - 1) / 2
+CHIP_ORDER = (4, 5, 6, 7, 0, 1, 2, 3)
+BLOCK_ORDER = (10, 11, 8, 9, 14, 15, 12, 13, 2, 3, 0, 1, 6, 7, 4, 5)
 
 
 def make_tables():
@@ -54,15 +56,17 @@
     for q in range(16):
         for s in range(2):
             for chip in range(Z_CHIPS):
-                theta = turn * freq[2 * chip + ((q % 2) ^ s)] * (16 * q + np.arange(16))
+                theta = turn * freq[2 * CHIP_ORDER[chip] + ((q % 2) ^ s)] * (16 * q + np.arange(16))
                 row = s * Z_CHIPS + chip
                 forward_y[q, row, 0] = (np.cos(theta) * scale)[None, :]
                 forward_y[q, row, 1] = (np.sin(theta) * scale)[None, :]
                 inverse_y[q, :, 0, row] = np.cos(theta)[:, None]
                 inverse_y[q, :, 1, row] = -np.sin(theta)[:, None]
 
-    phase = turn * np.outer(freq, 16 * np.arange(16) + CENTRE)
-    forward_x = np.stack([np.cos(phase), np.sin(phase)], axis=1)
+    order = list(BLOCK_ORDER)
+    phase = turn * np.outer(freq[order], 16 * np.arange(16) + CENTRE)
+    weight = weight[:, order]
+    forward_x = np.stack([np.cos(phase), np.sin(phase)], axis=1)[..., order]
     forward_x = np.repeat(forward_x[..., None], CHANNELS, axis=3).reshape(16, 512)
     lanes_v = np.tile(np.repeat(weight.T, MODES, axis=1), (1, 2))
     inverse_x = np.zeros((16, 2, RANK, 2, MODES))
@@ -326,7 +330,8 @@
 ANY = pl.BlockSpec(memory_space=pl.ANY)
 PARAMS = pltpu.CompilerParams(vmem_limit_bytes=VMEM)
 PAIR = [(i, i ^ 1) for i in range(16)]
-CHIPS = [list(range(0, 16, 2)), list(range(1, 16, 2))]
+CHIPS = [[2 * chip + core for chip in CHIP_ORDER] for core in range(2)]
+BLOCKS = [list(BLOCK_ORDER)]
 
 
 def shape_of(shape, dtype):
@@ -389,7 +394,7 @@
         out_shape=shape_of((16, 64, LANES), bf16),
         compiler_params=PARAMS,
     )(sums, packed)
-    message = lax.all_to_all(message, "px", 0, 0, tiled=True)
+    message = lax.all_to_all(message, "px", 0, 0, axis_index_groups=BLOCKS, tiled=True)
     message = pl.pallas_call(
         mix_kernel,
         name="mix",

time: 59.8 us -> 53.3 us (0.89)
  blocking collectives: 41.2 us -> 36.7 us
  starting transfers between devices: 6.91 us -> 4.98 us
    all_to_all x1, blocking collectives: 14.1 us -> 11.2 us  [on_device(): sums = lax.all_to_all(sums, 'py', 0, 0, axis_index_groups=CHIPS, tiled=True)]
    ppermute x1, starting transfers between devices: 3.58 us -> 1.65 us  [on_device(): other = lax.ppermute(own, 'py', PAIR)]
    all_to_all x1, blocking collectives: 15.9 us -> 14.8 us  [on_device(): lax.all_to_all(message, 'px', 0, 0, axis_index_groups=BLOCKS, tiled=True)]
where the time goes in v6:
time: 53.3 us; the launch traced here: 53 us
  blocking collectives  36.7 us (69%)
  Pallas kernels  10 us (19%)
  starting transfers between devices  4.98 us (9%)
  waiting for transfers between devices  1.17 us (2%)
    all_to_all x1, blocking collectives, on_device(): lax.all_to_all(message, 'px', 0, 0, axis_index_groups=BLOCKS, tiled=True)  14.8 us
    all_to_all x1, blocking collectives, on_device(): sums = lax.all_to_all(sums, 'py', 0, 0, axis_index_groups=CHIPS, tiled=True)  11.2 us
    all_to_all x1, blocking collectives, on_device(): lax.all_to_all(message, 'py', 0, 0, axis_index_groups=CHIPS, tiled=True)  10.7 us
    pallas_call x1, Pallas kernels, on_device(): pl.pallas_call(forward_kernel, name='forward', in_specs=[SM] + [ANY] * 6,...  4.53 us
    pallas_call x1, Pallas kernels, on_device(): pl.pallas_call(inverse_kernel, name='inverse', in_specs=[VM] * (7 + GROUP...  3.63 us
    ppermute x1, starting transfers between devices, on_device(): got = lax.ppermute(send, 'py', PAIR)  3.33 us
    ppermute x1, starting transfers between devices, on_device(): other = lax.ppermute(own, 'py', PAIR)  1.65 us
  transfers between devices with their start and end apart: 2, of which 2 were waited for; matrix products, arithmetic and copies ran while one was open for 0% of the time, Pallas kernels for 1%

profile of v6, /device:TPU:1, one launch (start us, length us, event | category | flops | bytes accessed | tf_op | source)
XLA Modules:
  0.0 53.0 jit_solution(15166902276655812586)
XLA Ops:
  0.0 0.0 copy-start
  0.0 0.1 pad_add_fusion.index_ref
  0.1 0.0 copy-start.1
  0.1 0.0 copy-start.2
  0.1 0.0 copy-start.3
  0.1 0.0 copy-start.4
  0.1 0.0 copy-start.5
  0.1 0.0 copy-start.6
  0.1 4.5 %forward.1 = (bf16[2,256,256]{2,1,0:T(8,128)(2,1)S(1)}, bf16[8,2,16,256]{3,2,1,0:T(8,128)(2,1)S(1)}, f32[16,512]{1,0:T(8,128)S(1)}, f32[16,512]{1,0:T(8,128)S(1)...) custom-call(s32[2]{0:T(128)S(1)} %pad_add_fusion.index_ref, ...), custom_call_target="tpu_custom_call" | custom-call | tf_op jit(solution)/shard_map/forward/pallas_call | solution.py:355
  4.7 3.3 %collective-permute-start = (bf16[8,2,16,256]{3,2,1,0:T(8,128)(2,1)S(1)}, bf16[8,2,16,256]{3,2,1,0:T(8,128)(2,1)S(1)}, u32[]{:S(2)}, u32[]{:S(2)}) collective-permute-start(bf16[8,2,16,256]{3,2,1,0:T(8,128)(2,1)S(1)} %get-tuple-element.29), channel_id=1, source_target_pairs={{0,1},{1,0},{2,3},{3,2},{4,5},{5,4},{6,7},{7,6},{8,9},{9,8},{10,11... | collective-permute-start | bytes 393224 | tf_op jit(solution)/shard_map/ppermute | solution.py:377
  8.0 0.0 copy-done
  8.0 0.5 keep.1
  8.5 0.5 collective-permute-done
  9.0 11.2 %all_to_all.15.parts_ref = bf16[8,2,16,256]{3,2,1,0:T(8,128)(2,1)S(1)} all-to-all(bf16[8,2,16,256]{3,2,1,0:T(8,128)(2,1)S(1)} %add_convert_fusion), channel_id=1, replica_groups={{8,10,12,14,0,2,4,6},{9,11,13,15,1,3,5,7},{24,26,28,30,16,18,20,22},{25..., dimensions={0} | all-to-all | bytes 262144 | tf_op jit(solution)/shard_map/all_to_all | solution.py:388
  20.2 14.8 %all_to_all.16.got_ref = bf16[16,64,256]{2,1,0:T(8,128)(2,1)S(1)} all-to-all(bf16[16,64,256]{2,1,0:T(8,128)(2,1)S(1)} %sum.1), channel_id=1, replica_groups={{160,176,128,144,224,240,192,208,32,48,0,16,96,112,64,80},{161,177,129,..., dimensions={0} | all-to-all | bytes 1048576 | tf_op jit(solution)/shard_map/all_to_all | solution.py:397
  35.1 0.0 copy-done.1
  35.1 0.0 copy-done.2
  35.1 1.0 %mix.1 = bf16[8,2,16,256]{3,2,1,0:T(8,128)(2,1)S(1)} custom-call(bf16[16,64,256]{2,1,0:T(8,128)(2,1)S(1)} %all_to_all.16.got_ref, f32[16,512]{1,0:T(8,128)S(1)} %copy-done.1, f32[16,256]{1,0:T(8,128)S(1)} %copy-done.2, f32[16,32]{1,0:T(8,128)S(1)} %get-tuple-element.31.back_x_ref), custom_call_target="tpu_custom_call" | custom-call | tf_op jit(solution)/shard_map/mix/pallas_call | solution.py:398
  36.1 10.7 %all_to_all.17.own_ref = bf16[8,2,16,256]{3,2,1,0:T(8,128)(2,1)S(1)} all-to-all(bf16[8,2,16,256]{3,2,1,0:T(8,128)(2,1)S(1)} %mix.1), channel_id=1, replica_groups={{8,10,12,14,0,2,4,6},{9,11,13,15,1,3,5,7},{24,26,28,30,16,18,20,22},{25..., dimensions={0} | all-to-all | bytes 262144 | tf_op jit(solution)/shard_map/all_to_all | solution.py:406
  46.8 1.6 %collective-permute-start.1 = (bf16[8,2,16,256]{3,2,1,0:T(8,128)(2,1)S(1)}, bf16[8,2,16,256]{3,2,1,0:T(8,128)(2,1)S(1)}, u32[]{:S(2)}, u32[]{:S(2)}) collective-permute-start(bf16[8,2,16,256]{3,2,1,0:T(8,128)(2,1)S(1)} %all_to_all.17.own_ref), channel_id=1, source_target_pairs={{0,1},{1,0},{2,3},{3,2},{4,5},{5,4},{6,7},{7,6},{8,9},{9,8},{10,11... | collective-permute-start | bytes 393224 | tf_op jit(solution)/shard_map/ppermute | solution.py:407
  48.4 0.0 copy-done.3
  48.4 0.0 copy-done.4
  48.4 0.0 copy-done.5
  48.4 0.0 copy-done.6
  48.4 0.3 prepare.1
  48.7 0.7 %collective-permute-done.1.other_ref = bf16[8,2,16,256]{3,2,1,0:T(8,128)(2,1)S(1)} collective-permute-done((bf16[8,2,16,256]{3,2,1,0:T(8,128)(2,1)S(1)}, bf16[8,2,16,256]{3,2,1,0:T(8,128)(2,1)S(1)}, u32[]{:S(2)}, u32[]{:S(2)}) %collective-permute-start.1) | collective-permute-done | bytes 131104 | tf_op jit(solution)/shard_map/ppermute | solution.py:407
  49.4 3.6 %inverse.1 = bf16[2,16,16,16,256]{4,3,2,1,0:T(8,128)(2,1)} custom-call(bf16[2,16,4,16,256]{4,3,2,1,0:T(8,128)(2,1)S(1)} %get-tuple-element.22.held0, bf16[2,16,4,16,256]{4,3,2,1,0:T(8,128)(2,1)S(1)} %get-tuple-element.23.held1, bf16[2,16,4,16,256]{4,3,2,1,0:T(8,128)(2,1)S(1)} %get-tuple-element.24.held2, ...), custom_call_target="tpu_custom_call" | custom-call | tf_op jit(solution)/shard_map/inverse/pallas_call | solution.py:424
  (2 shorter events, 0.1 us)
Async XLA Ops:
  0.0 8.0 %copy-start = (f32[1,1,2,16,16,16]{5,4,3,2,1,0:T(8,128)S(1)}, f32[1,1,2,16,16,16]{5,4,3,2,1,0:T(8,128)}, u32[]{:S(2)}) copy-start(f32[1,1,2,16,16,16]{5,4,3,2,1,0:T(8,128)} %param.14) | copy-start | bytes 98308
  0.1 35.0 %copy-start.1 = (f32[16,512]{1,0:T(8,128)S(1)}, f32[16,512]{1,0:T(8,128)}, u32[]{:S(2)}) copy-start(f32[16,512]{1,0:T(8,128)} %constant.30.clone.table_x_ref) | copy-start | bytes 98308
  0.1 35.0 %copy-start.2 = (f32[16,256]{1,0:T(8,128)S(1)}, f32[16,256]{1,0:T(8,128)}, u32[]{:S(2)}) copy-start(f32[16,256]{1,0:T(8,128)} %constant.31.clone.lanes_v_ref) | copy-start | bytes 49156
  0.1 48.3 %copy-start.3 = (bf16[16,16]{1,0:T(8,128)(2,1)S(1)}, bf16[16,16]{1,0:T(8,128)(2,1)}, u32[]{:S(2)}) copy-start(bf16[16,16]{1,0:T(8,128)(2,1)} %skip_ref.1) | copy-start | bytes 1540
  0.1 48.3 %copy-start.4 = (f32[16]{0:T(128)S(1)}, f32[16]{0:T(128)}, u32[]{:S(2)}) copy-start(f32[16]{0:T(128)} %param.16) | copy-start | bytes 196
  0.1 48.3 %copy-start.5 = (f32[32,256]{1,0:T(8,128)S(1)}, f32[32,256]{1,0:T(8,128)}, u32[]{:S(2)}) copy-start(f32[32,256]{1,0:T(8,128)} %constant.33.clone.table_z_ref) | copy-start | bytes 98308
  0.1 48.3 %copy-start.6 = (f32[16,512]{1,0:T(8,128)S(1)}, f32[16,512]{1,0:T(8,128)}, u32[]{:S(2)}) copy-start(f32[16,512]{1,0:T(8,128)} %constant.32.clone.basis_ref) | copy-start | bytes 98308
  4.7 4.3 %collective-permute-start = (bf16[8,2,16,256]{3,2,1,0:T(8,128)(2,1)S(1)}, bf16[8,2,16,256]{3,2,1,0:T(8,128)(2,1)S(1)}, u32[]{:S(2)}, u32[]{:S(2)}) collective-permute-start(bf16[8,2,16,256]{3,2,1,0:T(8,128)(2,1)S(1)} %get-tuple-element.29), channel_id=1, source_target_pairs={{0,1},{1,0},{2,3},{3,2},{4,5},{5,4},{6,7},{7,6},{8,9},{9,8},{10,11... | collective-permute-start | bytes 393224 | tf_op jit(solution)/shard_map/ppermute | solution.py:377
  46.8 2.6 %collective-permute-start.1 = (bf16[8,2,16,256]{3,2,1,0:T(8,128)(2,1)S(1)}, bf16[8,2,16,256]{3,2,1,0:T(8,128)(2,1)S(1)}, u32[]{:S(2)}, u32[]{:S(2)}) collective-permute-start(bf16[8,2,16,256]{3,2,1,0:T(8,128)(2,1)S(1)} %all_to_all.17.own_ref), channel_id=1, source_target_pairs={{0,1},{1,0},{2,3},{3,2},{4,5},{5,4},{6,7},{7,6},{8,9},{9,8},{10,11... | collective-permute-start | bytes 393224 | tf_op jit(solution)/shard_map/ppermute | solution.py:407
